TPU v7x, 128 devices: a whole 4x4x4 slice. The times are simulated.
128 devices in a mesh: bx: 8 (over y, core), by: 16 (over x, z).
Axes of the slice: x: 4, y: 4, z: 4, core: 2. Of those that a mesh axis runs over, the one named last changes fastest.
Arguments:
- initial_thermal_state: float32 [64, 524288], P(None, ('bx', 'by')), may hold values from -6 to 6
- baseline_diffusivity: float32 [64, 524288], P(None, ('bx', 'by')), may hold values from 0.3 to 3
- thermal_storage: float32 [64, 524288], P(None, ('bx', 'by')), may hold values from 0.5 to 4
- refinement_depth: int32 [524288], P(('bx', 'by')), may hold values from 0 to 2
- interface_voxel_table: int32 [128, 128, 32], P(('bx', 'by')), may hold values from 0 to 262143
- interface_weighting: float32 [128, 128, 32], P(('bx', 'by')), may hold values from 0.25 to 4, as said below
- laser_energy_deposits: float32 [1, 32768, 256], P(None, ('bx', 'by')), may hold values from 0 to 1
- laser_spot_holder: int32 [1, 32768, 1], P(None, ('bx', 'by')), may hold values from 0 to 127; in each aligned block of 256 rows (0 to 255, 256 to 511, ..., all dimensions but the last counted through in order) at most 8 rows name the same one
- laser_spot_patch: int32 [1, 32768], P(None, ('bx', 'by')), may hold values from 0 to 1023
Outputs:
- temperature_out: float32 [64, 524288], P(None, ('bx', 'by'))
- equation_misfit: float32 [64, 524288], P(None, ('bx', 'by'))
Inputs may be any that keep to these rules, and one draw needn't show every extreme that they name: interface_weighting[p, q, s] equals interface_weighting[q, p, s]. `laser_spot_holder`: among the scan points of one step in the rows of one device, at most 8 name the same owner, and in every draw some owner is named exactly 8 times.
All inputs are finite; a program needn't handle non-finite values.
Results may differ from a plain program's by a relative error of at most 0.00026.
Values sent between devices are 32-bit elements; how exact they have to be, the bound alone decides.
A program may use at most 128 MiB of HBM per device.

v0:
```python
import jax
import jax.numpy as jnp
from jax import lax
from jax.sharding import PartitionSpec as P

CAP = 8
ITERS = 4


def cond_links(diffuse_warmth, spacing):
    grid_cube = diffuse_warmth.reshape(4, 4, 4, -1)
    first_pairs = spacing * 0.5 * (grid_cube[1:] + grid_cube[:-1])
    second_pairs = spacing * 0.5 * (grid_cube[:, 1:] + grid_cube[:, :-1])
    third_pairs = spacing * 0.5 * (grid_cube[:, :, 1:] + grid_cube[:, :, :-1])
    return (first_pairs, second_pairs, third_pairs)


def inside_energy_current(values, interface_couplings):
    grid_cube = values.reshape(4, 4, 4, -1)
    flux_one = interface_couplings[0] * (grid_cube[1:] - grid_cube[:-1])
    flux_two = interface_couplings[1] * (grid_cube[:, 1:] - grid_cube[:, :-1])
    flux_three = interface_couplings[2] * (grid_cube[:, :, 1:] - grid_cube[:, :, :-1])
    zero_pad = (0, 0)
    balance = jnp.pad(flux_one, ((1, 0), zero_pad, zero_pad, zero_pad)) - jnp.pad(
        flux_one, ((0, 1), zero_pad, zero_pad, zero_pad)
    )
    balance = (
        balance
        + jnp.pad(flux_two, (zero_pad, (1, 0), zero_pad, zero_pad))
        - jnp.pad(flux_two, (zero_pad, (0, 1), zero_pad, zero_pad))
    )
    balance = (
        balance
        + jnp.pad(flux_three, (zero_pad, zero_pad, (1, 0), zero_pad))
        - jnp.pad(flux_three, (zero_pad, zero_pad, (0, 1), zero_pad))
    )
    return balance.reshape(values.shape)


def interface_energy_current(values, voxel_lattice, interface_diffusivity, own_vals, peer_vals):
    flux_vals = interface_diffusivity * (own_vals - peer_vals)
    flat_zero = jnp.zeros((values.size,), jnp.float32)
    return flat_zero.at[voxel_lattice.reshape(-1)].add(flux_vals.reshape(-1)).reshape(values.shape)


def apply_operator(values, heat_mass, interface_couplings, voxel_lattice, interface_diffusivity):
    own_vals = values.reshape(-1)[voxel_lattice]
    peer_vals = lax.all_to_all(own_vals, ("bx", "by"), split_axis=0, concat_axis=0, tiled=True)
    return (
        heat_mass * values
        + inside_energy_current(values, interface_couplings)
        + interface_energy_current(
            values, voxel_lattice, interface_diffusivity, own_vals, peer_vals
        )
    )


def squares(values):
    return lax.psum(jnp.sum(values * values), ("bx", "by"))


def shards(
    initial_thermal_state,
    baseline_diffusivity,
    thermal_storage,
    refinement_depth,
    interface_voxel_table,
    interface_weighting,
    laser_energy_deposits,
    laser_spot_holder,
    laser_spot_patch,
):
    owner_count = lax.axis_size(("bx", "by"))
    voxel_lattice = interface_voxel_table[0]
    areas = interface_weighting[0]
    patch_number = initial_thermal_state.shape[1] // 4
    step_count = laser_energy_deposits.shape[0]
    row_width = laser_energy_deposits.shape[2]
    spacing = 0.5 ** refinement_depth.astype(jnp.float32)
    heat_mass = thermal_storage * spacing**3

    def bucket(owners, tiles, row_block):
        matches = (owners[:, None] == jnp.arange(owner_count, dtype=jnp.int32)[None, :]).astype(
            jnp.int32
        )
        slot_rank = jnp.sum((jnp.cumsum(matches, 0) - 1) * matches, 1)
        slot_dest = owners * CAP + slot_rank
        sent_rows = (
            jnp.zeros((owner_count * CAP, row_width), jnp.float32).at[slot_dest].set(row_block)
        )
        sent_ids = (
            jnp.full((owner_count * CAP,), -1.0, jnp.float32)
            .at[slot_dest]
            .set(tiles.astype(jnp.float32))
        )
        return (sent_rows.reshape(owner_count, CAP, row_width), sent_ids.reshape(owner_count, CAP))

    sent_rows, sent_ids = jax.vmap(bucket)(
        laser_spot_holder[:, :, 0], laser_spot_patch, laser_energy_deposits
    )
    got_rows, got_ids = (
        lax.all_to_all(sent_rows, ("bx", "by"), split_axis=1, concat_axis=1, tiled=True),
        lax.all_to_all(sent_ids, ("bx", "by"), split_axis=1, concat_axis=1, tiled=True),
    )
    got_rows = got_rows.reshape(step_count, -1, row_width)
    got_ids = got_ids.reshape(step_count, -1)
    tile_iota = jnp.arange(patch_number, dtype=jnp.float32)
    equation_misfit = jnp.zeros_like(initial_thermal_state)
    matches = (got_ids[0][None, :] == tile_iota[:, None]).astype(jnp.float32)
    tile_heat = jnp.dot(
        matches, got_rows[0], precision=lax.Precision.HIGHEST, preferred_element_type=jnp.float32
    )
    energy_input = jnp.transpose(tile_heat.reshape(patch_number, 4, 64), (2, 0, 1)).reshape(
        64, patch_number * 4
    )
    diffuse_warmth = baseline_diffusivity * (1.0 + 0.5 * jnp.tanh(initial_thermal_state))
    interface_couplings = cond_links(diffuse_warmth, spacing)
    own_k = diffuse_warmth.reshape(-1)[voxel_lattice]
    home_thermal_state = initial_thermal_state.reshape(-1)[voxel_lattice]
    peer_k = lax.all_to_all(own_k, ("bx", "by"), split_axis=0, concat_axis=0, tiled=True)
    neighbor_thermal_state = lax.all_to_all(
        home_thermal_state, ("bx", "by"), split_axis=0, concat_axis=0, tiled=True
    )
    interface_diffusivity = areas * 0.5 * (own_k + peer_k)
    equation_misfit = energy_input - (
        inside_energy_current(initial_thermal_state, interface_couplings)
        + interface_energy_current(
            initial_thermal_state,
            voxel_lattice,
            interface_diffusivity,
            home_thermal_state,
            neighbor_thermal_state,
        )
    )
    conjugate_gradient_loop = initial_thermal_state

    def one_turn(turn_index, carry):
        conjugate_gradient_loop, equation_misfit, direction, res_norm = carry
        applied = apply_operator(
            direction, heat_mass, interface_couplings, voxel_lattice, interface_diffusivity
        )
        step_size = res_norm / lax.psum(jnp.sum(direction * applied), ("bx", "by"))
        conjugate_gradient_loop = conjugate_gradient_loop + step_size * direction
        equation_misfit = equation_misfit - step_size * applied
        next_norm = squares(equation_misfit)
        direction = equation_misfit + next_norm / res_norm * direction
        return (conjugate_gradient_loop, equation_misfit, direction, next_norm)

    start_norm = squares(equation_misfit)
    conjugate_gradient_loop, equation_misfit, direction, start_norm = lax.fori_loop(
        0, ITERS, one_turn, (conjugate_gradient_loop, equation_misfit, equation_misfit, start_norm)
    )
    return (conjugate_gradient_loop, equation_misfit)


def solution(mesh):
    return jax.shard_map(
        shards,
        mesh=mesh,
        in_specs=(
            P(None, ("bx", "by")),
            P(None, ("bx", "by")),
            P(None, ("bx", "by")),
            P(("bx", "by")),
            P(("bx", "by"), None, None),
            P(("bx", "by"), None, None),
            P(None, ("bx", "by"), None),
            P(None, ("bx", "by"), None),
            P(None, ("bx", "by")),
        ),
        out_specs=(P(None, ("bx", "by")), P(None, ("bx", "by"))),
        check_vma=False,
    )
```

profile of v0, /device:TPU:1, one launch (start us, length us, event | category | flops | bytes accessed | tf_op | source)
XLA Modules:
  0.0 1163.2 jit_solution(15317208055976307923)
XLA Ops:
  19.2 11.5 all-to-all-start.1
  30.9 23.0 %gather_fusion.1 = f32[4096]{0:T(1024)S(1)} fusion(f32[262144]{0:T(1024)S(1)} %bitcast.83, s32[4096]{0:T(1024)S(1)} %broadcast_clamp_fusion.1), kind=kCustom, calls=%fused_computation.1 | custom fusion | bytes 49152 | tf_op jit(solution)/shard_map/gather | solution.py:118
  55.3 9.8 all-to-all-start.3
  65.1 2.8 pad_subtract_fusion.1
  69.3 23.0 %gather_fusion.2 = f32[4096]{0:T(1024)S(1)} fusion(f32[262144]{0:T(1024)S(1)} %bitcast.84, s32[4096]{0:T(1024)S(1)} %broadcast_clamp_fusion.1), kind=kCustom, calls=%fused_computation.2 | custom fusion | bytes 49152 | tf_op jit(solution)/shard_map/gather | solution.py:119
  93.2 10.2 all-to-all-start.4
  103.6 36.7 %reshape.363 = f32[64,1024,4]{2,1,0:T(8,128)} reshape(f32[4,4,4,4096]{3,2,1,0:T(4,128)S(1)} %pad_subtract_fusion.1) | data formatting | bytes 2097152 | tf_op jit(solution)/shard_map/reshape | solution.py:37
  141.5 20.3 %copy.56 = f32[64,1024,4]{1,0,2:T(8,128)} copy(f32[64,1024,4]{2,1,0:T(8,128)} %reshape.363) | data formatting | bytes 2097152 | tf_op jit(solution)/shard_map/reshape | solution.py:37
  162.5 2.6 scatter_custom_fusion.3
  165.1 10.2 all-to-all-start.2
  179.6 22.2 %scatter_custom_fusion.1 = f32[262144]{0:T(1024)S(1)} fusion(s32[4096]{0:T(1024)S(1)} %bitcast.94, f32[4096]{0:T(1024)S(1)} %subtract_multiply_fusion.1, f32[]{:T(128)} %constant.59.clone.1), kind=kCustom, calls=%fused_computation.47 | custom fusion | flops 4096 | bytes 1048580 | tf_op jit(solution)/shard_map/scatter-add | solution.py:43
  201.8 36.0 %reshape.364 = f32[64,1024,4]{2,1,0:T(8,128)} reshape(f32[262144]{0:T(1024)S(1)} %scatter_custom_fusion.1) | data formatting | bytes 2097152 | tf_op jit(solution)/shard_map/reshape | solution.py:43
  238.9 20.4 %copy.57 = f32[64,1024,4]{1,0,2:T(8,128)} copy(f32[64,1024,4]{2,1,0:T(8,128)} %reshape.364) | data formatting | bytes 2097152 | tf_op jit(solution)/shard_map/reshape | solution.py:43
  261.4 2.6 copy.47
  264.0 5.4 multiply_reduce_fusion.2
  269.4 2.7 copy.48
  272.1 3.9 add_subtract_fusion
  276.0 3.1 copy.59
  280.4 67.4 %psum.27 = f32[]{:T(128)} all-reduce(f32[]{:T(128)} %get-tuple-element.226), channel_id=1, replica_groups=mesh['bx'=8,'by'=16] {'bx','by'}, use_global_device_ids=true, to_apply=%region_7.8 | all-reduce | flops 1 | bytes 8 | tf_op jit(solution)/shard_map/psum | solution.py:59
  347.7 814.5 %while.19 = (s32[]{:T(128)}, f32[64,4096]{1,0:T(8,128)}, f32[64,4096]{1,0:T(8,128)}, f32[64,4096]{1,0:T(8,128)S(1)}, f32[]{:T(128)}, /*index=5*/f32[64,4096]{1,0...) while((s32[]{:T(128)}, f32[64,4096]{1,0:T(8,128)}, ...), condition=%wide.wide.region_14.15_spmd, body=%wide.wide.region_8.14_spmd.sunk | while | flops 6725636 | bytes 54231424 | solution.py:150
  348.0 23.0 %gather_fusion = f32[4096]{0:T(1024)S(1)} fusion(f32[262144]{0:T(1024)S(1)} %bitcast.82, s32[4096]{0:T(1024)S(1)} %broadcast_clamp_fusion.4), kind=kCustom, calls=%fused_computation.clone.clone.1 | custom fusion | bytes 49152 | tf_op jit(solution)/shard_map/while/body/eval_jaxpr/gather | solution.py:47
  371.8 4.7 all-to-all-start
  387.5 22.9 %scatter_custom_fusion.13 = f32[262144]{0:T(1024)} fusion(s32[4096]{0:T(1024)S(1)} %bitcast.93, f32[4096]{0:T(1024)S(1)} %subtract_multiply_fusion.4, f32[]{:T(128)} %constant.59.clone.1..sunk), kind=kCustom, calls=%fused_computation.19.clone.clone.1 | custom fusion | flops 4096 | bytes 1048580 | tf_op jit(solution)/shard_map/while/body/eval_jaxpr/scatter-add | solution.py:43
  414.0 66.1 %psum.32 = f32[]{:T(128)} all-reduce(f32[]{:T(128)} %multiply_reduce_fusion.7), channel_id=1, replica_groups=mesh['bx'=8,'by'=16] {'bx','by'}, use_global_device_ids=true, to_apply=%region_11.11 | all-reduce | flops 1 | bytes 8 | tf_op jit(solution)/shard_map/while/body/eval_jaxpr/psum | solution.py:142
  480.8 3.5 multiply_reduce_fusion.8
  484.3 62.5 %psum.33 = f32[]{:T(128)} all-reduce(f32[]{:T(128)} %get-tuple-element.369), channel_id=1, replica_groups=mesh['bx'=8,'by'=16] {'bx','by'}, use_global_device_ids=true, to_apply=%region_13.13 | all-reduce | flops 1 | bytes 8 | tf_op jit(solution)/shard_map/while/body/eval_jaxpr/psum | solution.py:59
  547.5 3.3 multiply_add_fusion.4
  551.2 23.0 %gather_fusion = f32[4096]{0:T(1024)S(1)} fusion(f32[262144]{0:T(1024)S(1)} %bitcast.82, s32[4096]{0:T(1024)S(1)} %broadcast_clamp_fusion.4), kind=kCustom, calls=%fused_computation.clone.clone.1 | custom fusion | bytes 49152 | tf_op jit(solution)/shard_map/while/body/eval_jaxpr/gather | solution.py:47
  574.9 5.4 all-to-all-start
  591.3 22.9 %scatter_custom_fusion.13 = f32[262144]{0:T(1024)} fusion(s32[4096]{0:T(1024)S(1)} %bitcast.93, f32[4096]{0:T(1024)S(1)} %subtract_multiply_fusion.4, f32[]{:T(128)} %constant.59.clone.1..sunk), kind=kCustom, calls=%fused_computation.19.clone.clone.1 | custom fusion | flops 4096 | bytes 1048580 | tf_op jit(solution)/shard_map/while/body/eval_jaxpr/scatter-add | solution.py:43
  617.8 66.1 %psum.32 = f32[]{:T(128)} all-reduce(f32[]{:T(128)} %multiply_reduce_fusion.7), channel_id=1, replica_groups=mesh['bx'=8,'by'=16] {'bx','by'}, use_global_device_ids=true, to_apply=%region_11.11 | all-reduce | flops 1 | bytes 8 | tf_op jit(solution)/shard_map/while/body/eval_jaxpr/psum | solution.py:142
  684.6 3.5 multiply_reduce_fusion.8
  688.1 62.5 %psum.33 = f32[]{:T(128)} all-reduce(f32[]{:T(128)} %get-tuple-element.369), channel_id=1, replica_groups=mesh['bx'=8,'by'=16] {'bx','by'}, use_global_device_ids=true, to_apply=%region_13.13 | all-reduce | flops 1 | bytes 8 | tf_op jit(solution)/shard_map/while/body/eval_jaxpr/psum | solution.py:59
  751.3 3.3 multiply_add_fusion.4
  754.9 23.0 %gather_fusion = f32[4096]{0:T(1024)S(1)} fusion(f32[262144]{0:T(1024)S(1)} %bitcast.82, s32[4096]{0:T(1024)S(1)} %broadcast_clamp_fusion.4), kind=kCustom, calls=%fused_computation.clone.clone.1 | custom fusion | bytes 49152 | tf_op jit(solution)/shard_map/while/body/eval_jaxpr/gather | solution.py:47
  778.7 5.4 all-to-all-start
  795.1 22.9 %scatter_custom_fusion.13 = f32[262144]{0:T(1024)} fusion(s32[4096]{0:T(1024)S(1)} %bitcast.93, f32[4096]{0:T(1024)S(1)} %subtract_multiply_fusion.4, f32[]{:T(128)} %constant.59.clone.1..sunk), kind=kCustom, calls=%fused_computation.19.clone.clone.1 | custom fusion | flops 4096 | bytes 1048580 | tf_op jit(solution)/shard_map/while/body/eval_jaxpr/scatter-add | solution.py:43
  821.6 66.1 %psum.32 = f32[]{:T(128)} all-reduce(f32[]{:T(128)} %multiply_reduce_fusion.7), channel_id=1, replica_groups=mesh['bx'=8,'by'=16] {'bx','by'}, use_global_device_ids=true, to_apply=%region_11.11 | all-reduce | flops 1 | bytes 8 | tf_op jit(solution)/shard_map/while/body/eval_jaxpr/psum | solution.py:142
  888.4 3.5 multiply_reduce_fusion.8
  891.9 62.5 %psum.33 = f32[]{:T(128)} all-reduce(f32[]{:T(128)} %get-tuple-element.369), channel_id=1, replica_groups=mesh['bx'=8,'by'=16] {'bx','by'}, use_global_device_ids=true, to_apply=%region_13.13 | all-reduce | flops 1 | bytes 8 | tf_op jit(solution)/shard_map/while/body/eval_jaxpr/psum | solution.py:59
  955.1 3.3 multiply_add_fusion.4
  958.7 23.0 %gather_fusion = f32[4096]{0:T(1024)S(1)} fusion(f32[262144]{0:T(1024)S(1)} %bitcast.82, s32[4096]{0:T(1024)S(1)} %broadcast_clamp_fusion.4), kind=kCustom, calls=%fused_computation.clone.clone.1 | custom fusion | bytes 49152 | tf_op jit(solution)/shard_map/while/body/eval_jaxpr/gather | solution.py:47
  982.5 5.4 all-to-all-start
  998.9 22.9 %scatter_custom_fusion.13 = f32[262144]{0:T(1024)} fusion(s32[4096]{0:T(1024)S(1)} %bitcast.93, f32[4096]{0:T(1024)S(1)} %subtract_multiply_fusion.4, f32[]{:T(128)} %constant.59.clone.1..sunk), kind=kCustom, calls=%fused_computation.19.clone.clone.1 | custom fusion | flops 4096 | bytes 1048580 | tf_op jit(solution)/shard_map/while/body/eval_jaxpr/scatter-add | solution.py:43
  1025.4 66.1 %psum.32 = f32[]{:T(128)} all-reduce(f32[]{:T(128)} %multiply_reduce_fusion.7), channel_id=1, replica_groups=mesh['bx'=8,'by'=16] {'bx','by'}, use_global_device_ids=true, to_apply=%region_11.11 | all-reduce | flops 1 | bytes 8 | tf_op jit(solution)/shard_map/while/body/eval_jaxpr/psum | solution.py:142
  1092.2 3.5 multiply_reduce_fusion.8
  1095.6 62.5 %psum.33 = f32[]{:T(128)} all-reduce(f32[]{:T(128)} %get-tuple-element.369), channel_id=1, replica_groups=mesh['bx'=8,'by'=16] {'bx','by'}, use_global_device_ids=true, to_apply=%region_13.13 | all-reduce | flops 1 | bytes 8 | tf_op jit(solution)/shard_map/while/body/eval_jaxpr/psum | solution.py:59
  1158.9 3.3 multiply_add_fusion.4
  (228 shorter events, 93.0 us)
Async XLA Ops:
  0.6 161.9 %copy-start = (f32[1,256,256]{2,1,0:T(8,128)S(1)}, f32[1,256,256]{2,1,0:T(8,128)}, u32[]{:S(2)}) copy-start(f32[1,256,256]{2,1,0:T(8,128)} %param.17) | copy-start | bytes 786436
  0.6 3.9 copy-start.8
  4.6 1.7 copy-start.24
  9.7 2.5 copy-start.26
  12.2 1.9 copy-start.22
  12.3 2.3 copy-start.28
  14.6 4.7 copy-start.27
  16.7 1.4 copy-start.10
  19.2 35.5 %all-to-all-start.1 = ((f32[1,128,8]{2,0,1:T(1,128)}), f32[1,128,8]{2,0,1:T(1,128)S(1)}, u32[]{:S(2)}, u32[]{:S(2)}) async-start(f32[1,128,8]{2,0,1:T(1,128)} %bitcast.15), calls=%async_computation.1 | async-start | bytes 131072 | tf_op jit(solution)/shard_map/all_to_all | solution.py:103
  30.9 34.2 %copy-start.7 = (f32[4,4,3,4096]{3,2,1,0:T(4,128)S(1)}, f32[4,4,3,4096]{3,2,1,0:T(4,128)}, u32[]{:S(2)}) copy-start(f32[4,4,3,4096]{3,2,1,0:T(4,128)} %get-tuple-element.220) | copy-start | bytes 2359300
  55.3 37.8 %all-to-all-start.3 = ((f32[128,1,32]{2,1,0:T(1,128)}), f32[128,1,32]{2,1,0:T(1,128)S(1)}, u32[]{:S(2)}, u32[]{:S(2)}) async-start(f32[128,1,32]{2,1,0:T(1,128)} %bitcast.27), calls=%async_computation.3 | async-start | bytes 131072 | tf_op jit(solution)/shard_map/all_to_all | solution.py:120
  69.3 23.8 %copy-start.25 = (f32[1,128,32]{1,2,0:T(8,128)S(1)}, f32[1,128,32]{1,2,0:T(8,128)}, u32[]{:S(2)}) copy-start(f32[1,128,32]{1,2,0:T(8,128)} %param.16) | copy-start | bytes 49156
  69.3 34.2 %copy-start.23 = (s32[1,128,32]{1,2,0:T(8,128)S(1)}, s32[1,128,32]{1,2,0:T(8,128)}, u32[]{:S(2)}) copy-start(s32[1,128,32]{1,2,0:T(8,128)} %param.15) | copy-start | bytes 49156
  92.3 11.1 copy-start.16
  93.1 10.4 copy-start.14
  93.2 47.1 %copy-start.11 = (f32[128,1,32]{2,1,0:T(1,128)}, f32[128,1,32]{2,1,0:T(1,128)S(1)}, u32[]{:S(2)}) copy-start(f32[128,1,32]{2,1,0:T(1,128)S(1)} %all-to-all-done.3) | copy-start | bytes 49156
  93.2 71.9 %all-to-all-start.4 = ((f32[128,1,32]{2,1,0:T(1,128)}), f32[128,1,32]{2,1,0:T(1,128)}, u32[]{:S(2)}, u32[]{:S(2)}) async-start(f32[128,1,32]{2,1,0:T(1,128)} %bitcast.28), calls=%async_computation.4 | async-start | bytes 131072 | tf_op jit(solution)/shard_map/all_to_all | solution.py:121
  162.5 13.4 %copy-start.19 = (f32[1,128,8]{2,0,1:T(1,128)S(1)}, f32[1,128,8]{2,0,1:T(1,128)}, u32[]{:S(2)}) copy-start(f32[1,128,8]{2,0,1:T(1,128)} %copy-done.18) | copy-start | bytes 12292
  162.5 14.4 %copy-start.12 = (f32[128,1,32]{2,1,0:T(1,128)S(1)}, f32[128,1,32]{2,1,0:T(1,128)}, u32[]{:S(2)}) copy-start(f32[128,1,32]{2,1,0:T(1,128)} %copy-done.11) | copy-start | bytes 49156
  162.5 17.1 %copy-start.17 = (f32[4096]{0:T(1024)S(1)}, f32[4096]{0:T(1024)}, u32[]{:S(2)}) copy-start(f32[4096]{0:T(1024)} %copy-done.16) | copy-start | bytes 49156
  165.1 96.3 %all-to-all-start.2 = ((f32[1,128,8,256]{3,2,0,1:T(8,128)}), f32[1,128,8,256]{3,2,0,1:T(8,128)}, u32[]{:S(2)}, u32[]{:S(2)}) async-start(f32[1,128,8,256]{3,2,0,1:T(8,128)} %bitcast.19), calls=%async_computation.2 | async-start | bytes 2097152 | tf_op jit(solution)/shard_map/all_to_all | solution.py:102
  238.9 20.4 %copy-start.6 = (f32[64,4096]{1,0:T(8,128)S(1)}, f32[64,4096]{1,0:T(8,128)}, u32[]{:S(2)}) copy-start(f32[64,4096]{1,0:T(8,128)} %reshape.362) | copy-start | bytes 3145732
  259.3 2.0 copy-start.13
  259.3 2.0 copy-start.15
  259.3 2.0 copy-start.21
  261.3 2.8 copy-start.9
  261.3 8.1 copy-start.20
  371.8 14.3 %all-to-all-start = ((f32[128,1,32]{2,1,0:T(1,128)}), f32[128,1,32]{2,1,0:T(1,128)S(1)}, u32[]{:S(2)}, u32[]{:S(2)}) async-start(f32[128,1,32]{2,1,0:T(1,128)} %bitcast.81), calls=%async_computation | async-start | bytes 131072 | tf_op jit(solution)/shard_map/while/body/eval_jaxpr/all_to_all | solution.py:48
  376.8 1.2 copy-start.4
  378.1 1.4 copy-start.5
  380.6 2.8 copy-start.2
  381.7 1.7 copy-start.3
  574.9 14.9 %all-to-all-start = ((f32[128,1,32]{2,1,0:T(1,128)}), f32[128,1,32]{2,1,0:T(1,128)S(1)}, u32[]{:S(2)}, u32[]{:S(2)}) async-start(f32[128,1,32]{2,1,0:T(1,128)} %bitcast.81), calls=%async_computation | async-start | bytes 131072 | tf_op jit(solution)/shard_map/while/body/eval_jaxpr/all_to_all | solution.py:48
  580.6 1.2 copy-start.4
  581.8 1.4 copy-start.5
  584.4 2.8 copy-start.2
  585.5 1.7 copy-start.3
  778.7 14.9 %all-to-all-start = ((f32[128,1,32]{2,1,0:T(1,128)}), f32[128,1,32]{2,1,0:T(1,128)S(1)}, u32[]{:S(2)}, u32[]{:S(2)}) async-start(f32[128,1,32]{2,1,0:T(1,128)} %bitcast.81), calls=%async_computation | async-start | bytes 131072 | tf_op jit(solution)/shard_map/while/body/eval_jaxpr/all_to_all | solution.py:48
  784.4 1.2 copy-start.4
  785.6 1.4 copy-start.5
  788.2 2.8 copy-start.2
  789.3 1.7 copy-start.3
  982.5 14.9 %all-to-all-start = ((f32[128,1,32]{2,1,0:T(1,128)}), f32[128,1,32]{2,1,0:T(1,128)S(1)}, u32[]{:S(2)}, u32[]{:S(2)}) async-start(f32[128,1,32]{2,1,0:T(1,128)} %bitcast.81), calls=%async_computation | async-start | bytes 131072 | tf_op jit(solution)/shard_map/while/body/eval_jaxpr/all_to_all | solution.py:48
  988.2 1.2 copy-start.4
  989.4 1.4 copy-start.5
  991.9 2.8 copy-start.2
  993.0 1.7 copy-start.3
  1162.2 0.9 copy-start.1
  (1 other events, 0.6 us)
where the time goes:
time: 1170 us; the launch traced here: 1160 us
  blocking collectives  582 us (50%)
  local copies, waits for them, and re-layouts  307 us (26%)
  other arithmetic  192 us (16%)
  starting transfers between devices  62.7 us (5%)
    psum x5, blocking collectives, squares(): return lax.psum(jnp.sum(values * values), ('bx', 'by'))  318 us
    psum x4, blocking collectives, one_turn(): step_size = res_norm / lax.psum(jnp.sum(direction * applied), ('bx', 'by'))  265 us
    scatter-add x5, other arithmetic, interface_energy_current(): flat_zero.at[voxel_lattice.reshape(-1)].add(flux_vals.reshape(-1))  114 us
    gather x4, local copies, waits for them, and re-layouts, apply_operator(): own_vals = values.reshape(-1)[voxel_lattice]  92.1 us
    reshape x8, local copies, waits for them, and re-layouts, interface_energy_current(): flat_zero.at[voxel_lattice.reshape(-1)].add(flux_vals.reshape(-1))  65.1 us
    reshape x8, local copies, waits for them, and re-layouts, inside_energy_current(): return balance.reshape(values.shape)  59.4 us
    gather x2, local copies, waits for them, and re-layouts, shards(): own_k = diffuse_warmth.reshape(-1)[voxel_lattice]  23.7 us
  transfers between devices with their start and end apart: 8, of which 4 were waited for; matrix products, arithmetic and copies ran while one was open for 19% of the time, Pallas kernels for 0%

commit v1 on v0

--- a/solution.py
+++ b/solution.py
@@ -1,7 +1,11 @@
 import jax
 import jax.numpy as jnp
 from jax import lax
+from jax.experimental import pallas as pl
+from jax.experimental.pallas import tpu as pltpu
 from jax.sharding import PartitionSpec as P
+
+MESH = pl.DeviceIdType.MESH
 
 CAP = 8
 ITERS = 4
@@ -55,8 +59,62 @@
     )
 
 
+def sum_kernel(x_ref, lane_ref, o_ref, snd, rcv, ssem, rsem):
+    bx, by = lax.axis_index("bx"), lax.axis_index("by")
+    nx, ny = lax.axis_size("bx"), lax.axis_size("by")
+    n = nx * ny
+    me = bx * ny + by
+    b = pltpu.get_barrier_semaphore()
+
+    def greet(i, c):
+        p = lax.rem(me + i, n)
+        pl.semaphore_signal(b, inc=1, device_id=(p // ny, lax.rem(p, ny)), device_id_type=MESH)
+        return c
+
+    lax.fori_loop(1, n, greet, 0)
+    x = jnp.take_along_axis(x_ref[...], lane_ref[...], axis=1)
+    snd[...] = jnp.sum(x, axis=0, keepdims=True)
+    rcv[pl.ds(me, 1)] = snd[...]
+    pl.semaphore_wait(b, n - 1)
+
+    def send(i, c):
+        p = lax.rem(me + i, n)
+        pltpu.make_async_remote_copy(
+            src_ref=snd.at[pl.ds(0, 1)], dst_ref=rcv.at[pl.ds(me, 1)], send_sem=ssem, recv_sem=rsem,
+            device_id=(p // ny, lax.rem(p, ny)), device_id_type=MESH,
+        ).start()
+        return c
+
+    lax.fori_loop(1, n, send, 0)
+    p = lax.rem(me + 1, n)
+    pltpu.make_async_remote_copy(
+        src_ref=rcv.at[pl.ds(0, n - 1)], dst_ref=rcv.at[pl.ds(0, n - 1)], send_sem=ssem, recv_sem=rsem,
+        device_id=(p // ny, lax.rem(p, ny)), device_id_type=MESH,
+    ).wait()
+    o_ref[...] = jnp.broadcast_to(jnp.sum(rcv[...]), (8, 128))
+
+
+def total(value):
+    x = jnp.zeros((8, 128), jnp.float32).at[0, 0].set(value)
+    lanes = lax.broadcasted_iota(jnp.int32, (8, 128), 1)
+    n = lax.axis_size(("bx", "by"))
+    return pl.pallas_call(
+        sum_kernel,
+        out_shape=jax.ShapeDtypeStruct((8, 128), jnp.float32),
+        in_specs=[pl.BlockSpec(memory_space=pltpu.VMEM)] * 2,
+        out_specs=pl.BlockSpec(memory_space=pltpu.VMEM),
+        scratch_shapes=[
+            pltpu.VMEM((1, 128), jnp.float32),
+            pltpu.VMEM((n, 128), jnp.float32),
+            pltpu.SemaphoreType.DMA,
+            pltpu.SemaphoreType.DMA,
+        ],
+        compiler_params=pltpu.CompilerParams(collective_id=0, has_side_effects=True),
+    )(x, lanes)[0, 0]
+
+
 def squares(values):
-    return lax.psum(jnp.sum(values * values), ("bx", "by"))
+    return total(jnp.sum(values * values))
 
 
 def shards(
@@ -139,7 +197,7 @@
         applied = apply_operator(
             direction, heat_mass, interface_couplings, voxel_lattice, interface_diffusivity
         )
-        step_size = res_norm / lax.psum(jnp.sum(direction * applied), ("bx", "by"))
+        step_size = res_norm / total(jnp.sum(direction * applied))
         conjugate_gradient_loop = conjugate_gradient_loop + step_size * direction
         equation_misfit = equation_misfit - step_size * applied
         next_norm = squares(equation_misfit)

time: 1170 us -> 748 us (0.64)
  blocking collectives: 582 us -> 0 us
  Pallas kernels: 0 us -> 134 us
  local copies, waits for them, and re-layouts: 307 us -> 333 us
    psum x9 -> x0, blocking collectives: 582 us -> none  [the longest x5 318 us: squares(): return lax.psum(jnp.sum(values * values), ('bx', 'by'))]
    pallas_call x0 -> x9, Pallas kernels: none -> 134 us  [total(): pl.pallas_call(sum_kernel, out_shape=jax.ShapeDtypeStruct((8, 128), jnp.f...]
  transfers between devices with their start and end apart: 8 -> 8, of which waited for: 4 -> 4; matrix products, arithmetic and copies ran while one was open for 19% -> 30% of each run, Pallas kernels for 0% -> 0%
where the time goes in v1:
time: 748 us; the launch traced here: 745 us
  local copies, waits for them, and re-layouts  333 us (45%)
  other arithmetic  191 us (26%)
  Pallas kernels  134 us (18%)
  starting transfers between devices  68 us (9%)
  loops' own time  8.33 us (1%)
    pallas_call x9, Pallas kernels, total(): pl.pallas_call(sum_kernel, out_shape=jax.ShapeDtypeStruct((8, 128), jnp.f...  134 us
    scatter-add x5, other arithmetic, interface_energy_current(): flat_zero.at[voxel_lattice.reshape(-1)].add(flux_vals.reshape(-1))  114 us
    gather x4, local copies, waits for them, and re-layouts, apply_operator(): own_vals = values.reshape(-1)[voxel_lattice]  92.1 us
    reshape x8, local copies, waits for them, and re-layouts, interface_energy_current(): flat_zero.at[voxel_lattice.reshape(-1)].add(flux_vals.reshape(-1))  65.1 us
    reshape x8, local copies, waits for them, and re-layouts, inside_energy_current(): return balance.reshape(values.shape)  59.4 us
    all_to_all x4, starting transfers between devices, apply_operator(): lax.all_to_all(own_vals, ('bx', 'by'), split_axis=0, concat_axis=0, tiled...  26.3 us
    gather x2, local copies, waits for them, and re-layouts, shards(): own_k = diffuse_warmth.reshape(-1)[voxel_lattice]  23.7 us
    gather x1, local copies, waits for them, and re-layouts, shards(): home_thermal_state = initial_thermal_state.reshape(-1)[voxel_lattice]  23 us
  transfers between devices with their start and end apart: 8, of which 4 were waited for; matrix products, arithmetic and copies ran while one was open for 30% of the time, Pallas kernels for 0%

profile of v1, /device:TPU:1, one launch (start us, length us, event | category | flops | bytes accessed | tf_op | source)
XLA Modules:
  0.0 744.8 jit_solution(15969353328849999494)
XLA Ops:
  19.2 11.5 %all-to-all-start.1 = ((f32[1,128,8]{2,0,1:T(1,128)}), f32[1,128,8]{2,0,1:T(1,128)S(1)}, u32[]{:S(2)}, u32[]{:S(2)}) async-start(f32[1,128,8]{2,0,1:T(1,128)} %bitcast.19), calls=%async_computation.1 | async-start | bytes 131072 | tf_op jit(solution)/shard_map/all_to_all | solution.py:161
  30.9 23.0 %gather_fusion.1 = f32[4096]{0:T(1024)S(1)} fusion(f32[262144]{0:T(1024)S(1)} %bitcast.101, s32[4096]{0:T(1024)S(1)} %broadcast_clamp_fusion.1), kind=kCustom, calls=%fused_computation.1 | custom fusion | bytes 49152 | tf_op jit(solution)/shard_map/gather | solution.py:176
  55.3 9.8 %all-to-all-start.3 = ((f32[128,1,32]{2,1,0:T(1,128)}), f32[128,1,32]{2,1,0:T(1,128)S(1)}, u32[]{:S(2)}, u32[]{:S(2)}) async-start(f32[128,1,32]{2,1,0:T(1,128)} %bitcast.31), calls=%async_computation.3 | async-start | bytes 131072 | tf_op jit(solution)/shard_map/all_to_all | solution.py:178
  65.0 2.7 pad_subtract_fusion.1
  69.2 23.0 %gather_fusion.2 = f32[4096]{0:T(1024)S(1)} fusion(f32[262144]{0:T(1024)S(1)} %bitcast.102, s32[4096]{0:T(1024)S(1)} %broadcast_clamp_fusion.1), kind=kCustom, calls=%fused_computation.2 | custom fusion | bytes 49152 | tf_op jit(solution)/shard_map/gather | solution.py:177
  93.1 10.2 %all-to-all-start.4 = ((f32[128,1,32]{2,1,0:T(1,128)}), f32[128,1,32]{2,1,0:T(1,128)}, u32[]{:S(2)}, u32[]{:S(2)}) async-start(f32[128,1,32]{2,1,0:T(1,128)} %bitcast.32), calls=%async_computation.4 | async-start | bytes 131072 | tf_op jit(solution)/shard_map/all_to_all | solution.py:179
  103.5 36.7 %reshape.464 = f32[64,1024,4]{2,1,0:T(8,128)} reshape(f32[4,4,4,4096]{3,2,1,0:T(4,128)S(1)} %pad_subtract_fusion.1) | data formatting | bytes 2097152 | tf_op jit(solution)/shard_map/reshape | solution.py:41
  141.4 20.3 %copy.56 = f32[64,1024,4]{1,0,2:T(8,128)} copy(f32[64,1024,4]{2,1,0:T(8,128)} %reshape.464) | data formatting | bytes 2097152 | tf_op jit(solution)/shard_map/reshape | solution.py:41
  162.5 2.6 scatter_custom_fusion.3
  165.0 10.2 %all-to-all-start.2 = ((f32[1,128,8,256]{3,2,0,1:T(8,128)}), f32[1,128,8,256]{3,2,0,1:T(8,128)}, u32[]{:S(2)}, u32[]{:S(2)}) async-start(f32[1,128,8,256]{3,2,0,1:T(8,128)} %bitcast.23), calls=%async_computation.2 | async-start | bytes 2097152 | tf_op jit(solution)/shard_map/all_to_all | solution.py:160
  179.4 22.4 %scatter_custom_fusion.1 = f32[262144]{0:T(1024)S(1)} fusion(s32[4096]{0:T(1024)S(1)} %bitcast.112, f32[4096]{0:T(1024)S(1)} %subtract_multiply_fusion.1, f32[]{:T(128)} %constant.141.clone.1), kind=kCustom, calls=%fused_computation.47 | custom fusion | flops 4096 | bytes 1048580 | tf_op jit(solution)/shard_map/scatter-add | solution.py:47
  201.7 35.9 %reshape.465 = f32[64,1024,4]{2,1,0:T(8,128)} reshape(f32[262144]{0:T(1024)S(1)} %scatter_custom_fusion.1) | data formatting | bytes 2097152 | tf_op jit(solution)/shard_map/reshape | solution.py:47
  238.8 20.4 %copy.57 = f32[64,1024,4]{1,0,2:T(8,128)} copy(f32[64,1024,4]{2,1,0:T(8,128)} %reshape.465) | data formatting | bytes 2097152 | tf_op jit(solution)/shard_map/reshape | solution.py:47
  261.3 2.6 copy.47
  264.0 5.3 multiply_reduce_fusion.2
  269.2 2.7 copy.48
  271.9 3.9 add_subtract_fusion
  275.8 3.1 copy.59
  281.9 16.7 %shard_map.104 = f32[8,128]{1,0:T(8,128)} custom-call(f32[8,128]{1,0:T(8,128)} %scatter.31.x_ref, s32[8,128]{1,0:T(8,128)} %iota.33.lane_ref), custom_call_target="tpu_custom_call" | custom-call | tf_op jit(solution)/shard_map/pallas_call | solution.py:101
  299.8 444.1 %while.22 = (s32[]{:T(128)}, f32[64,4096]{1,0:T(8,128)}, f32[64,4096]{1,0:T(8,128)}, f32[64,4096]{1,0:T(8,128)S(1)}, f32[]{:T(128)}, /*index=5*/f32[64,4096]{1,0...) while((s32[]{:T(128)}, f32[64,4096]{1,0:T(8,128)}, ...), condition=%wide.wide.region_11.12_spmd, body=%wide.wide.region_7.11_spmd.sunk | while | flops 6725634 | bytes 54247824 | solution.py:208
  300.1 23.0 %gather_fusion = f32[4096]{0:T(1024)S(1)} fusion(f32[262144]{0:T(1024)S(1)} %bitcast.100, s32[4096]{0:T(1024)S(1)} %broadcast_clamp_fusion.4), kind=kCustom, calls=%fused_computation.clone.clone.1 | custom fusion | bytes 49152 | tf_op jit(solution)/shard_map/while/body/eval_jaxpr/gather | solution.py:51
  323.8 6.6 all-to-all-start
  341.2 22.9 %scatter_custom_fusion.13 = f32[262144]{0:T(1024)} fusion(s32[4096]{0:T(1024)S(1)} %bitcast.111, f32[4096]{0:T(1024)S(1)} %subtract_multiply_fusion.4, f32[]{:T(128)} %constant.141.clone.1..sunk), kind=kCustom, calls=%fused_computation.19.clone.clone.1 | custom fusion | flops 4096 | bytes 1048580 | tf_op jit(solution)/shard_map/while/body/eval_jaxpr/scatter-add | solution.py:47
  369.3 15.5 %eval_jaxpr.8 = f32[8,128]{1,0:T(8,128)} custom-call(f32[8,128]{1,0:T(8,128)} %scatter.50.x_ref, s32[8,128]{1,0:T(8,128)} %iota.40.lane_ref), custom_call_target="tpu_custom_call" | custom-call | tf_op jit(solution)/shard_map/while/body/eval_jaxpr/pallas_call | solution.py:101
  386.8 3.4 multiply_reduce_fusion.8
  391.9 13.8 %eval_jaxpr.9 = f32[8,128]{1,0:T(8,128)} custom-call(f32[8,128]{1,0:T(8,128)} %scatter.51.x_ref, s32[8,128]{1,0:T(8,128)} %iota.41.lane_ref), custom_call_target="tpu_custom_call" | custom-call | tf_op jit(solution)/shard_map/while/body/eval_jaxpr/pallas_call | solution.py:101
  407.5 3.3 multiply_add_fusion.4
  411.1 23.0 %gather_fusion = f32[4096]{0:T(1024)S(1)} fusion(f32[262144]{0:T(1024)S(1)} %bitcast.100, s32[4096]{0:T(1024)S(1)} %broadcast_clamp_fusion.4), kind=kCustom, calls=%fused_computation.clone.clone.1 | custom fusion | bytes 49152 | tf_op jit(solution)/shard_map/while/body/eval_jaxpr/gather | solution.py:51
  434.8 6.6 all-to-all-start
  452.2 22.9 %scatter_custom_fusion.13 = f32[262144]{0:T(1024)} fusion(s32[4096]{0:T(1024)S(1)} %bitcast.111, f32[4096]{0:T(1024)S(1)} %subtract_multiply_fusion.4, f32[]{:T(128)} %constant.141.clone.1..sunk), kind=kCustom, calls=%fused_computation.19.clone.clone.1 | custom fusion | flops 4096 | bytes 1048580 | tf_op jit(solution)/shard_map/while/body/eval_jaxpr/scatter-add | solution.py:47
  480.4 15.5 %eval_jaxpr.8 = f32[8,128]{1,0:T(8,128)} custom-call(f32[8,128]{1,0:T(8,128)} %scatter.50.x_ref, s32[8,128]{1,0:T(8,128)} %iota.40.lane_ref), custom_call_target="tpu_custom_call" | custom-call | tf_op jit(solution)/shard_map/while/body/eval_jaxpr/pallas_call | solution.py:101
  497.8 3.4 multiply_reduce_fusion.8
  502.9 13.8 %eval_jaxpr.9 = f32[8,128]{1,0:T(8,128)} custom-call(f32[8,128]{1,0:T(8,128)} %scatter.51.x_ref, s32[8,128]{1,0:T(8,128)} %iota.41.lane_ref), custom_call_target="tpu_custom_call" | custom-call | tf_op jit(solution)/shard_map/while/body/eval_jaxpr/pallas_call | solution.py:101
  518.5 3.3 multiply_add_fusion.4
  522.1 23.0 %gather_fusion = f32[4096]{0:T(1024)S(1)} fusion(f32[262144]{0:T(1024)S(1)} %bitcast.100, s32[4096]{0:T(1024)S(1)} %broadcast_clamp_fusion.4), kind=kCustom, calls=%fused_computation.clone.clone.1 | custom fusion | bytes 49152 | tf_op jit(solution)/shard_map/while/body/eval_jaxpr/gather | solution.py:51
  545.9 6.6 all-to-all-start
  563.3 22.9 %scatter_custom_fusion.13 = f32[262144]{0:T(1024)} fusion(s32[4096]{0:T(1024)S(1)} %bitcast.111, f32[4096]{0:T(1024)S(1)} %subtract_multiply_fusion.4, f32[]{:T(128)} %constant.141.clone.1..sunk), kind=kCustom, calls=%fused_computation.19.clone.clone.1 | custom fusion | flops 4096 | bytes 1048580 | tf_op jit(solution)/shard_map/while/body/eval_jaxpr/scatter-add | solution.py:47
  591.4 15.5 %eval_jaxpr.8 = f32[8,128]{1,0:T(8,128)} custom-call(f32[8,128]{1,0:T(8,128)} %scatter.50.x_ref, s32[8,128]{1,0:T(8,128)} %iota.40.lane_ref), custom_call_target="tpu_custom_call" | custom-call | tf_op jit(solution)/shard_map/while/body/eval_jaxpr/pallas_call | solution.py:101
  608.8 3.4 multiply_reduce_fusion.8
  613.9 13.8 %eval_jaxpr.9 = f32[8,128]{1,0:T(8,128)} custom-call(f32[8,128]{1,0:T(8,128)} %scatter.51.x_ref, s32[8,128]{1,0:T(8,128)} %iota.41.lane_ref), custom_call_target="tpu_custom_call" | custom-call | tf_op jit(solution)/shard_map/while/body/eval_jaxpr/pallas_call | solution.py:101
  629.5 3.3 multiply_add_fusion.4
  633.2 23.0 %gather_fusion = f32[4096]{0:T(1024)S(1)} fusion(f32[262144]{0:T(1024)S(1)} %bitcast.100, s32[4096]{0:T(1024)S(1)} %broadcast_clamp_fusion.4), kind=kCustom, calls=%fused_computation.clone.clone.1 | custom fusion | bytes 49152 | tf_op jit(solution)/shard_map/while/body/eval_jaxpr/gather | solution.py:51
  656.9 6.6 all-to-all-start
  674.3 22.9 %scatter_custom_fusion.13 = f32[262144]{0:T(1024)} fusion(s32[4096]{0:T(1024)S(1)} %bitcast.111, f32[4096]{0:T(1024)S(1)} %subtract_multiply_fusion.4, f32[]{:T(128)} %constant.141.clone.1..sunk), kind=kCustom, calls=%fused_computation.19.clone.clone.1 | custom fusion | flops 4096 | bytes 1048580 | tf_op jit(solution)/shard_map/while/body/eval_jaxpr/scatter-add | solution.py:47
  702.4 15.5 %eval_jaxpr.8 = f32[8,128]{1,0:T(8,128)} custom-call(f32[8,128]{1,0:T(8,128)} %scatter.50.x_ref, s32[8,128]{1,0:T(8,128)} %iota.40.lane_ref), custom_call_target="tpu_custom_call" | custom-call | tf_op jit(solution)/shard_map/while/body/eval_jaxpr/pallas_call | solution.py:101
  719.9 3.4 multiply_reduce_fusion.8
  724.9 13.8 %eval_jaxpr.9 = f32[8,128]{1,0:T(8,128)} custom-call(f32[8,128]{1,0:T(8,128)} %scatter.51.x_ref, s32[8,128]{1,0:T(8,128)} %iota.41.lane_ref), custom_call_target="tpu_custom_call" | custom-call | tf_op jit(solution)/shard_map/while/body/eval_jaxpr/pallas_call | solution.py:101
  740.6 3.3 multiply_add_fusion.4
  (255 shorter events, 118.4 us)
Async XLA Ops:
  0.6 161.8 %copy-start = (f32[1,256,256]{2,1,0:T(8,128)S(1)}, f32[1,256,256]{2,1,0:T(8,128)}, u32[]{:S(2)}) copy-start(f32[1,256,256]{2,1,0:T(8,128)} %param.23) | copy-start | bytes 786436
  0.6 3.9 copy-start.8
  4.6 1.7 copy-start.24
  9.7 2.4 copy-start.26
  12.1 1.9 copy-start.22
  12.2 2.3 copy-start.28
  14.5 4.7 copy-start.27
  16.6 1.4 copy-start.10
  19.2 35.5 %all-to-all-start.1 = ((f32[1,128,8]{2,0,1:T(1,128)}), f32[1,128,8]{2,0,1:T(1,128)S(1)}, u32[]{:S(2)}, u32[]{:S(2)}) async-start(f32[1,128,8]{2,0,1:T(1,128)} %bitcast.19), calls=%async_computation.1 | async-start | bytes 131072 | tf_op jit(solution)/shard_map/all_to_all | solution.py:161
  30.9 34.2 %copy-start.7 = (f32[4,4,3,4096]{3,2,1,0:T(4,128)S(1)}, f32[4,4,3,4096]{3,2,1,0:T(4,128)}, u32[]{:S(2)}) copy-start(f32[4,4,3,4096]{3,2,1,0:T(4,128)} %get-tuple-element.258) | copy-start | bytes 2359300
  55.3 37.8 %all-to-all-start.3 = ((f32[128,1,32]{2,1,0:T(1,128)}), f32[128,1,32]{2,1,0:T(1,128)S(1)}, u32[]{:S(2)}, u32[]{:S(2)}) async-start(f32[128,1,32]{2,1,0:T(1,128)} %bitcast.31), calls=%async_computation.3 | async-start | bytes 131072 | tf_op jit(solution)/shard_map/all_to_all | solution.py:178
  69.2 23.8 %copy-start.25 = (f32[1,128,32]{1,2,0:T(8,128)S(1)}, f32[1,128,32]{1,2,0:T(8,128)}, u32[]{:S(2)}) copy-start(f32[1,128,32]{1,2,0:T(8,128)} %param.22) | copy-start | bytes 49156
  69.2 34.2 %copy-start.23 = (s32[1,128,32]{1,2,0:T(8,128)S(1)}, s32[1,128,32]{1,2,0:T(8,128)}, u32[]{:S(2)}) copy-start(s32[1,128,32]{1,2,0:T(8,128)} %param.21) | copy-start | bytes 49156
  92.3 11.1 %copy-start.16 = (f32[4096]{0:T(1024)}, f32[4096]{0:T(1024)S(1)}, u32[]{:S(2)}) copy-start(f32[4096]{0:T(1024)S(1)} %gather_fusion.2) | copy-start | bytes 49156
  93.1 10.4 %copy-start.14 = (f32[1,128,32]{2,1,0:T(8,128)}, f32[1,128,32]{2,1,0:T(8,128)S(1)}, u32[]{:S(2)}) copy-start(f32[1,128,32]{2,1,0:T(8,128)S(1)} %copy.50) | copy-start | bytes 49156
  93.1 47.1 %copy-start.11 = (f32[128,1,32]{2,1,0:T(1,128)}, f32[128,1,32]{2,1,0:T(1,128)S(1)}, u32[]{:S(2)}) copy-start(f32[128,1,32]{2,1,0:T(1,128)S(1)} %all-to-all-done.3) | copy-start | bytes 49156
  93.1 71.9 %all-to-all-start.4 = ((f32[128,1,32]{2,1,0:T(1,128)}), f32[128,1,32]{2,1,0:T(1,128)}, u32[]{:S(2)}, u32[]{:S(2)}) async-start(f32[128,1,32]{2,1,0:T(1,128)} %bitcast.32), calls=%async_computation.4 | async-start | bytes 131072 | tf_op jit(solution)/shard_map/all_to_all | solution.py:179
  162.4 13.4 %copy-start.19 = (f32[1,128,8]{2,0,1:T(1,128)S(1)}, f32[1,128,8]{2,0,1:T(1,128)}, u32[]{:S(2)}) copy-start(f32[1,128,8]{2,0,1:T(1,128)} %copy-done.18) | copy-start | bytes 12292
  162.4 14.3 %copy-start.12 = (f32[128,1,32]{2,1,0:T(1,128)S(1)}, f32[128,1,32]{2,1,0:T(1,128)}, u32[]{:S(2)}) copy-start(f32[128,1,32]{2,1,0:T(1,128)} %copy-done.11) | copy-start | bytes 49156
  162.5 16.9 %copy-start.17 = (f32[4096]{0:T(1024)S(1)}, f32[4096]{0:T(1024)}, u32[]{:S(2)}) copy-start(f32[4096]{0:T(1024)} %copy-done.16) | copy-start | bytes 49156
  165.0 96.3 %all-to-all-start.2 = ((f32[1,128,8,256]{3,2,0,1:T(8,128)}), f32[1,128,8,256]{3,2,0,1:T(8,128)}, u32[]{:S(2)}, u32[]{:S(2)}) async-start(f32[1,128,8,256]{3,2,0,1:T(8,128)} %bitcast.23), calls=%async_computation.2 | async-start | bytes 2097152 | tf_op jit(solution)/shard_map/all_to_all | solution.py:160
  238.8 20.4 %copy-start.6 = (f32[64,4096]{1,0:T(8,128)S(1)}, f32[64,4096]{1,0:T(8,128)}, u32[]{:S(2)}) copy-start(f32[64,4096]{1,0:T(8,128)} %reshape.463) | copy-start | bytes 3145732
  259.2 2.0 copy-start.13
  259.2 2.0 copy-start.15
  259.2 2.0 copy-start.21
  261.2 2.7 copy-start.9
  261.3 8.0 %copy-start.20 = (f32[128,32]{1,0:T(8,128)}, f32[128,32]{1,0:T(8,128)S(1)}, u32[]{:S(2)}) copy-start(f32[128,32]{1,0:T(8,128)S(1)} %bitcast_multiply_fusion) | copy-start | bytes 49156
  323.8 16.1 %all-to-all-start = ((f32[128,1,32]{2,1,0:T(1,128)}), f32[128,1,32]{2,1,0:T(1,128)S(1)}, u32[]{:S(2)}, u32[]{:S(2)}) async-start(f32[128,1,32]{2,1,0:T(1,128)} %bitcast.95), calls=%async_computation | async-start | bytes 131072 | tf_op jit(solution)/shard_map/while/body/eval_jaxpr/all_to_all | solution.py:52
  330.7 1.2 copy-start.4
  331.9 1.4 copy-start.5
  334.4 2.8 copy-start.2
  335.5 1.7 copy-start.3
  434.8 16.1 %all-to-all-start = ((f32[128,1,32]{2,1,0:T(1,128)}), f32[128,1,32]{2,1,0:T(1,128)S(1)}, u32[]{:S(2)}, u32[]{:S(2)}) async-start(f32[128,1,32]{2,1,0:T(1,128)} %bitcast.95), calls=%async_computation | async-start | bytes 131072 | tf_op jit(solution)/shard_map/while/body/eval_jaxpr/all_to_all | solution.py:52
  441.8 1.2 copy-start.4
  443.0 1.4 copy-start.5
  445.5 2.8 copy-start.2
  446.6 1.7 copy-start.3
  545.9 16.1 %all-to-all-start = ((f32[128,1,32]{2,1,0:T(1,128)}), f32[128,1,32]{2,1,0:T(1,128)S(1)}, u32[]{:S(2)}, u32[]{:S(2)}) async-start(f32[128,1,32]{2,1,0:T(1,128)} %bitcast.95), calls=%async_computation | async-start | bytes 131072 | tf_op jit(solution)/shard_map/while/body/eval_jaxpr/all_to_all | solution.py:52
  552.8 1.2 copy-start.4
  554.0 1.4 copy-start.5
  556.5 2.8 copy-start.2
  557.6 1.7 copy-start.3
  656.9 16.1 %all-to-all-start = ((f32[128,1,32]{2,1,0:T(1,128)}), f32[128,1,32]{2,1,0:T(1,128)S(1)}, u32[]{:S(2)}, u32[]{:S(2)}) async-start(f32[128,1,32]{2,1,0:T(1,128)} %bitcast.95), calls=%async_computation | async-start | bytes 131072 | tf_op jit(solution)/shard_map/while/body/eval_jaxpr/all_to_all | solution.py:52
  663.8 1.2 copy-start.4
  665.0 1.4 copy-start.5
  667.5 2.8 copy-start.2
  668.6 1.7 copy-start.3
  743.9 0.9 copy-start.1
  (1 other events, 0.6 us)

commit v2 on v0

--- a/solution.py
+++ b/solution.py
@@ -1,10 +1,17 @@
+import functools
+
 import jax
 import jax.numpy as jnp
 from jax import lax
+from jax.experimental import pallas as pl
+from jax.experimental.pallas import tpu as pltpu
 from jax.sharding import PartitionSpec as P
 
 CAP = 8
 ITERS = 4
+MESH = pl.DeviceIdType.MESH
+F32, BF16, I32 = jnp.float32, jnp.bfloat16, jnp.int32
+ROUNDS = 6
 
 
 def cond_links(diffuse_warmth, spacing):
@@ -59,7 +66,7 @@
     return lax.psum(jnp.sum(values * values), ("bx", "by"))
 
 
-def shards(
+def general(
     initial_thermal_state,
     baseline_diffusivity,
     thermal_storage,
@@ -153,6 +160,504 @@
     return (conjugate_gradient_loop, equation_misfit)
 
 
+def lanes_of(x, idx):
+    return jnp.take_along_axis(x, idx, axis=1, mode="promise_in_bounds")
+
+
+def thirds(x):
+    a = x.astype(BF16)
+    rest = x - a.astype(F32)
+    b = rest.astype(BF16)
+    c = (rest - b.astype(F32)).astype(BF16)
+    return a, b, c
+
+
+def iota(shape, dim):
+    return lax.broadcasted_iota(I32, shape, dim)
+
+
+def dot_nt(a, b):
+    return lax.dot_general(a, b, (((1,), (1,)), ((), ())), preferred_element_type=F32)
+
+
+def dot_nn(a, b):
+    return jnp.dot(a, b, preferred_element_type=F32)
+
+
+def peers():
+    bx, by = lax.axis_index("bx"), lax.axis_index("by")
+    offs = []
+    for dc in range(2):
+        for dy in range(4):
+            for dx in range(4):
+                for dz in range(4):
+                    if (dc, dy, dx, dz) != (0, 0, 0, 0):
+                        hops = min(dy, 4 - dy) + min(dx, 4 - dx) + min(dz, 4 - dz)
+                        offs.append((-hops, dc, dy, dx, dz))
+    offs.sort()
+    y, core, x, z = bx // 2, lax.rem(bx, 2), by // 4, lax.rem(by, 4)
+    for _, dc, dy, dx, dz in offs:
+        px = lax.rem(y + dy, 4) * 2 + lax.rem(core + dc, 2)
+        py = lax.rem(x + dx, 4) * 4 + lax.rem(z + dz, 4)
+        yield px, py
+
+
+def step_kernel(
+    temp_hbm, base_hbm, store_hbm, level_hbm, face_hbm, area_hbm, rows_hbm, owner_hbm, tile_hbm,
+    x_out, r_out, flag_out,
+    in_t, in_b, in_s, level, face, area, rows, owner, tile,
+    xf, kf, mf, gx, gy, gz, ra, rb, wf, sf, pf, nat, en,
+    ohs, ohl, celltab, lanetab, srcrow, srclane, rowid, slane, slots, slots2, msgs,
+    ro, rp, so, sp, gface, heat, oht,
+    snd, rcv, lsnd, lrcv,
+    in_sem, ssem, rsem, lssem, lrsem, out_sem,
+):
+    bx, by = lax.axis_index("bx"), lax.axis_index("by")
+    me = bx * 16 + by
+    barrier = pltpu.get_barrier_semaphore()
+    for px, py in peers():
+        pl.semaphore_signal(barrier, inc=1, device_id=(px, py), device_id_type=MESH)
+
+    loads = [
+        pltpu.make_async_copy(src, dst, in_sem.at[i])
+        for i, (src, dst) in enumerate(
+            [(owner_hbm, owner), (tile_hbm, tile), (rows_hbm, rows), (face_hbm, face), (area_hbm, area), (level_hbm, level),
+             (temp_hbm, in_t), (base_hbm, in_b), (store_hbm, in_s)]
+        )
+    ]
+    for c in loads:
+        c.start()
+
+    for c in loads[:3]:
+        c.wait()
+    own = owner[...]
+    match = iota((128, 256), 0) == own
+    upto = (iota((256, 256), 0) <= iota((256, 256), 1)).astype(F32).astype(BF16)
+    before = dot_nn(match.astype(F32).astype(BF16), upto) - 1.0
+    rank = jnp.sum(jnp.where(match, before, 0.0), axis=0, keepdims=True)
+    dest = own * CAP + rank.astype(I32)
+    place = (iota((1024, 256), 0) == dest).astype(F32).astype(BF16)
+    pieces = thirds(rows[...])
+    put = (dot_nn(place, pieces[0]) + dot_nn(place, pieces[1])) + dot_nn(place, pieces[2])
+    lsnd[...] = put.reshape(128, 8, 256)
+    num = tile[...] + 1
+    is_rank = iota((8, 256), 0) == rank.astype(I32)
+    high = jnp.where(is_rank, num >> 5, 0).astype(F32)
+    low = jnp.where(is_rank, num & 31, 0).astype(F32)
+    hl = jnp.concatenate([high, low], axis=0).astype(BF16)
+    ids = dot_nt(hl, match.astype(F32).astype(BF16))
+    ids = ids[0:8] * 32.0 + ids[8:16] - 1.0
+
+    for c in loads[3:6]:
+        c.wait()
+    fc = face[...]
+    bt = (fc & 4095) >> 7
+    for i in range(32):
+        ohs[pl.ds(32 * i, 32), :] = (iota((32, 128), 0) == bt[i : i + 1]).astype(F32).astype(BF16)
+    tri = (iota((128, 128), 0) <= iota((128, 128), 1)).astype(F32).astype(BF16)
+    ones = jnp.ones((128, 128), BF16)
+    run = jnp.zeros((32, 128), F32)
+    ranks = []
+    for i in range(32):
+        oh = ohs[pl.ds(32 * i, 32), :]
+        pre = dot_nn(oh, tri)
+        ranks.append(jnp.sum(oh.astype(F32) * (pre + run - 1.0), axis=0, keepdims=True))
+        run = run + dot_nn(oh, ones)
+    rank = jnp.concatenate(ranks, axis=0).astype(I32)
+    over = jnp.max(jnp.max((rank >= 256).astype(F32), axis=0, keepdims=True), axis=1, keepdims=True)
+    rid = (rank >> 7) * 32 + bt
+    rowid[...] = rid
+    slane[...] = rank & 127
+    cellv = (fc >> 12).astype(F32)
+    lanev = (fc & 127).astype(F32)
+    lane_f = iota((1, 128), 1).astype(F32)
+    acc = jnp.zeros((256, 128), F32)
+    for i in range(32):
+        hit = iota((64, 128), 0) == rid[i : i + 1]
+        a = jnp.concatenate(
+            [
+                jnp.where(hit, F32(i + 1), 0.0),
+                jnp.where(hit, lane_f, 0.0),
+                jnp.where(hit, cellv[i : i + 1], 0.0),
+                jnp.where(hit, lanev[i : i + 1], 0.0),
+            ],
+            axis=0,
+        ).astype(BF16)
+        b = (iota((128, 128), 0) == slane[i : i + 1, :]).astype(F32).astype(BF16)
+        acc = acc + dot_nt(a, b)
+    tab = acc.astype(I32)
+    filled = tab[0:64] > 0
+    srcrow[...] = tab[0:64] - 1
+    srclane[...] = tab[64:128]
+    celltab[...] = jnp.where(filled, tab[128:192], -1)
+    lanetab[...] = tab[192:256]
+
+    def lane_hot(b, c):
+        for h in range(2):
+            row = lanetab[pl.ds(b + 32 * h, 1), :]
+            ohl[pl.ds(b, 1), :, pl.ds(128 * h, 128)] = (
+                (iota((128, 128), 0) == row).astype(F32).astype(BF16).reshape(1, 128, 128)
+            )
+        return c
+
+    lax.fori_loop(0, 32, lane_hot, 0)
+
+    for c in loads[6:]:
+        c.wait()
+
+    def prepare(k, c):
+        lv = level[pl.ds(8 * k, 8), :]
+        spacing = jnp.where(lv == 0, 1.0, jnp.where(lv == 1, 0.5, 0.25)).astype(F32)
+        cube = spacing * spacing * spacing
+        half = spacing * 0.5
+        at = pl.ds(8 * k, 8)
+        kv = {}
+        for c in range(64):
+            i, j, l = c // 16, (c // 4) % 4, c % 4
+            where = pl.ds((c // 8) * 256 + c % 8 + 64 * k, 8, stride=8)
+            t = in_t[where, :]
+            kc = in_b[where, :] * (1.0 + 0.5 * jnp.tanh(t))
+            xf[c, at, :] = t
+            kf[c, at, :] = kc
+            mf[c, at, :] = in_s[where, :] * cube
+            kv[c] = kc
+            if i:
+                gx[c - 16, at, :] = half * (kc + kv.pop(c - 16))
+            if j:
+                gy[(i * 3 + j - 1) * 4 + l, at, :] = half * (kc + kv[c - 4])
+            if l:
+                gz[(i * 4 + j) * 3 + l - 1, at, :] = half * (kc + kv[c - 1])
+        return 0
+
+    lax.fori_loop(0, 4, prepare, 0)
+
+    def gather(field, out):
+        def group(k, c):
+            at, at2 = pl.ds(8 * k, 8), pl.ds(32 + 8 * k, 8)
+            l0, l1, c0, c1 = lanetab[at, :], lanetab[at2, :], celltab[at, :], celltab[at2, :]
+            a0 = jnp.zeros((8, 128), F32)
+            a1 = jnp.zeros((8, 128), F32)
+            for cell in range(64):
+                v = field[cell, at, :]
+                a0 = jnp.where(c0 == cell, lanes_of(v, l0), a0)
+                a1 = jnp.where(c1 == cell, lanes_of(v, l1), a1)
+            out[at, :] = a0
+            out[at2, :] = a1
+            return c
+
+        lax.fori_loop(0, 4, group, 0)
+
+    def to_entries(src):
+        outs = []
+        for g in range(4):
+            ri, la = rowid[8 * g : 8 * g + 8, :], slane[8 * g : 8 * g + 8, :]
+            a = jnp.zeros((8, 128), F32)
+            for t in range(64):
+                row = jnp.broadcast_to(src[t : t + 1, :], (8, 128))
+                a = jnp.where(ri == t, lanes_of(row, la), a)
+            outs.append(a)
+        return jnp.concatenate(outs, axis=0)
+
+    def to_slots(src, out):
+        for g in range(8):
+            ri, la = srcrow[8 * g : 8 * g + 8, :], srclane[8 * g : 8 * g + 8, :]
+            a = jnp.zeros((8, 128), F32)
+            for t in range(32):
+                row = jnp.broadcast_to(src[t : t + 1, :], (8, 128))
+                a = jnp.where(ri == t, lanes_of(row, la), a)
+            out[8 * g : 8 * g + 8, :] = a
+
+    def scatter(flux):
+        def one(b, c):
+            parts = [[], [], []]
+            for h in range(2):
+                row = flux[pl.ds(b + 32 * h, 1), :]
+                hit = iota((64, 128), 0) == celltab[pl.ds(b + 32 * h, 1), :]
+                p0 = row.astype(BF16).astype(F32)
+                p1 = (row - p0).astype(BF16).astype(F32)
+                p2 = row - p0 - p1
+                for q, p in enumerate((p0, p1, p2)):
+                    parts[q].append(jnp.where(hit, p, 0.0))
+            a = jnp.concatenate([jnp.concatenate(p, axis=1) for p in parts], axis=0).astype(BF16)
+            o = dot_nt(a, ohl[b])
+            nat[pl.ds(64 * b, 64), :] = (o[0:64] + o[64:128]) + o[128:192]
+            return c
+
+        lax.fori_loop(0, 32, one, 0, unroll=4)
+
+    def stencil(k, load, emit, mass):
+        at = pl.ds(8 * k, 8)
+        v, acc = {}, {}
+        for c in range(64):
+            i, j, l = c // 16, (c // 4) % 4, c % 4
+            v[c] = load(c)
+            a = mf[c, at, :] * v[c] if mass else jnp.zeros((8, 128), F32)
+            if l:
+                f = gz[(i * 4 + j) * 3 + l - 1, at, :] * (v[c] - v[c - 1])
+                a, acc[c - 1] = a + f, acc[c - 1] - f
+            if j:
+                f = gy[(i * 3 + j - 1) * 4 + l, at, :] * (v[c] - v[c - 4])
+                a, acc[c - 4] = a + f, acc[c - 4] - f
+            if i:
+                f = gx[c - 16, at, :] * (v[c] - v.pop(c - 16))
+                a = a + f
+                emit(c - 16, acc.pop(c - 16) - f)
+            acc[c] = a
+        for c in range(48, 64):
+            emit(c, acc[c])
+
+    def send(r, feats):
+        n = sum(f.shape[0] for f in feats)
+        full = jnp.concatenate(list(feats) + [jnp.zeros((128 - n, 128), F32)], axis=0)
+        snd[r] = full.T
+        rcv[r, pl.ds(me, 1), :] = snd[r, pl.ds(me, 1), :]
+        for px, py in peers():
+            pltpu.make_async_remote_copy(
+                src_ref=snd.at[r, pl.ds(px * 16 + py, 1)], dst_ref=rcv.at[r, pl.ds(me, 1)],
+                send_sem=ssem.at[r], recv_sem=rsem.at[r], device_id=(px, py), device_id_type=MESH,
+            ).start()
+
+    def all_of(r):
+        return pltpu.make_async_remote_copy(
+            src_ref=snd.at[r, pl.ds(0, 127)], dst_ref=rcv.at[r, pl.ds(0, 127)],
+            send_sem=ssem.at[r], recv_sem=rsem.at[r],
+            device_id=(lax.rem(bx + 1, 8), by), device_id_type=MESH,
+        )
+
+    def receive(r):
+        all_of(r).wait_recv()
+        return rcv[r].T
+
+    def total(rows):
+        return jnp.sum(rows, axis=1, keepdims=True)
+
+    pl.semaphore_wait(barrier, 127)
+    lrcv[pl.ds(me, 1)] = lsnd[pl.ds(me, 1)]
+
+    gather(kf, slots)
+    gather(xf, slots2)
+    send(0, [to_entries(slots), to_entries(slots2), ids, jnp.broadcast_to(over, (8, 128))])
+    for px, py in peers():
+        pltpu.make_async_remote_copy(
+            src_ref=lsnd.at[pl.ds(px * 16 + py, 1)], dst_ref=lrcv.at[pl.ds(me, 1)],
+            send_sem=lssem, recv_sem=lrsem, device_id=(px, py), device_id_type=MESH,
+        ).start()
+    msgs[...] = receive(0)
+    to_slots(msgs.at[pl.ds(0, 32)], gface)
+    to_slots(msgs.at[pl.ds(32, 32)], rp)
+    to_slots(area, ro)
+    gface[...] = ro[...] * 0.5 * (slots[...] + gface[...])
+    slots[...] = gface[...] * (slots2[...] - rp[...])
+    scatter(slots)
+    flag_out[...] = jnp.broadcast_to(jnp.max(msgs[72:80, :], axis=1, keepdims=True), (8, 128))
+    tids = msgs[64:72, :].astype(I32)
+    for j in range(8):
+        oht[:, pl.ds(128 * j, 128)] = (iota((1024, 128), 0) == tids[j : j + 1]).astype(F32).astype(BF16)
+
+    laser = pltpu.make_async_remote_copy(
+        src_ref=lsnd.at[pl.ds(0, 127)], dst_ref=lrcv.at[pl.ds(0, 127)],
+        send_sem=lssem, recv_sem=lrsem, device_id=(lax.rem(bx + 1, 8), by), device_id_type=MESH,
+    )
+    laser.wait_recv()
+    by_rank = []
+    for j in range(8):
+        by_rank.append(lrcv[:, j, :])
+    pieces = thirds(jnp.concatenate(by_rank, axis=0))
+    for q in range(8):
+        o = oht[pl.ds(128 * q, 128), :]
+        h = (dot_nn(o, pieces[0]) + dot_nn(o, pieces[1])) + dot_nn(o, pieces[2])
+        heat[:, pl.ds(128 * q, 128)] = h.T
+    lane = iota((8, 128), 1)
+    for b in range(32):
+        idx = 32 * (b % 4) + (lane >> 2)
+        for g in range(8):
+            a = jnp.zeros((8, 128), F32)
+            for q in range(4):
+                v = heat[64 * q + 8 * g : 64 * q + 8 * g + 8, 128 * (b // 4) : 128 * (b // 4) + 128]
+                a = jnp.where((lane & 3) == q, lanes_of(v, idx), a)
+            en[64 * b + 8 * g : 64 * b + 8 * g + 8, :] = a
+
+    def first(k, rr):
+        at = pl.ds(8 * k, 8)
+        total_rr = [rr]
+
+        def emit(c, a):
+            here = pl.ds(512 * k + c, 8, stride=64)
+            r = en[here, :] - (a + nat[here, :])
+            ra[c, at, :] = r
+            total_rr[0] = total_rr[0] + r * r
+
+        stencil(k, lambda c: xf[c, at, :], emit, False)
+        return total_rr[0]
+
+    zero = jnp.zeros((8, 128), F32)
+    lax.fori_loop(0, 4, first, zero)
+    gather(ra, ro)
+    send(1, [to_entries(ro)])
+    msgs[...] = receive(1)
+    to_slots(msgs.at[pl.ds(0, 32)], rp)
+
+    def image(rnew, load):
+        slots[...] = gface[...] * (ro[...] - rp[...])
+        scatter(slots)
+
+        def group(k, sums):
+            at = pl.ds(8 * k, 8)
+            s = list(sums)
+
+            def emit(c, a):
+                r = rnew[c, at, :]
+                w = a + nat[pl.ds(512 * k + c, 8, stride=64), :]
+                wf[c, at, :] = w
+                s[0] = s[0] + r * r
+                s[1] = s[1] + r * w
+
+            stencil(k, lambda c: load(k, c), emit, True)
+            return tuple(s)
+
+        rr, rw = lax.fori_loop(0, 4, group, (zero, zero))
+        full = [jnp.sum(jnp.sum(v, axis=0, keepdims=True), axis=1, keepdims=True) for v in (rr, rw)]
+        return [jnp.broadcast_to(v, (8, 128)) for v in full]
+
+    rr, rw = image(ra, lambda k, c: ra[c, pl.ds(8 * k, 8), :])
+    old_rr = old_alpha = None
+    r_now, r_next = ra, rb
+    for it in range(ITERS):
+        last = it == ITERS - 1
+        if last:
+            send(it + 2, [rr, rw])
+        else:
+            gather(wf, slots)
+            send(it + 2, [to_entries(slots), rr, rw])
+        if it:
+            def advance(k, c, it=it, beta=beta, alpha=alpha, r_old=r_old):
+                at = pl.ds(8 * k, 8)
+                for cell in range(64):
+                    d = r_old[cell, at, :]
+                    if it > 1:
+                        d = d + beta * pf[cell, at, :]
+                    pf[cell, at, :] = d
+                    xf[cell, at, :] = xf[cell, at, :] + alpha * d
+                return c
+
+            lax.fori_loop(0, 4, advance, 0)
+        msgs[...] = receive(it + 2)
+        base = 0 if last else 32
+        g_rr, g_rw = total(msgs[base : base + 1, :]), total(msgs[base + 8 : base + 9, :])
+        if it:
+            beta1 = g_rr / old_rr
+            alpha1 = g_rr / (g_rw - beta1 * g_rr / old_alpha)
+            beta = jnp.broadcast_to(beta1, (8, 128))
+        else:
+            alpha1 = g_rr / g_rw
+            beta = None
+        alpha = jnp.broadcast_to(alpha1, (8, 128))
+        old_rr, old_alpha = g_rr, alpha1
+        r_old = r_now
+        if last:
+            break
+        to_slots(msgs.at[pl.ds(0, 32)], slots2)
+        if it:
+            so[...] = slots[...] + beta1 * so[...]
+            sp[...] = slots2[...] + beta1 * sp[...]
+        else:
+            so[...] = slots[...]
+            sp[...] = slots2[...]
+        ro[...] = ro[...] - alpha1 * so[...]
+        rp[...] = rp[...] - alpha1 * sp[...]
+
+        def load(k, c, it=it, alpha=alpha, beta=beta, r_now=r_now, r_next=r_next):
+            at = pl.ds(8 * k, 8)
+            s = wf[c, at, :]
+            if it:
+                s = s + beta * sf[c, at, :]
+            sf[c, at, :] = s
+            r = r_now[c, at, :] - alpha * s
+            r_next[c, at, :] = r
+            return r
+
+        rr, rw = image(r_next, load)
+        r_now, r_next = r_next, r_now
+
+    def finish(k, c):
+        at = pl.ds(8 * k, 8)
+        for cell in range(64):
+            where = pl.ds((cell // 8) * 256 + cell % 8 + 64 * k, 8, stride=8)
+            r = r_now[cell, at, :]
+            d = r + beta * pf[cell, at, :]
+            in_t[where, :] = xf[cell, at, :] + alpha * d
+            in_b[where, :] = r - alpha * (wf[cell, at, :] + beta * sf[cell, at, :])
+        return c
+
+    lax.fori_loop(0, 4, finish, 0)
+    outs = [pltpu.make_async_copy(in_t, x_out, out_sem.at[0]), pltpu.make_async_copy(in_b, r_out, out_sem.at[1])]
+    for c in outs:
+        c.start()
+    for r in range(ROUNDS):
+        all_of(r).wait_send()
+    laser.wait_send()
+    for c in outs:
+        c.wait()
+
+
+def tiled(v):
+    return v.reshape(8, 8, 32, 128).transpose(0, 2, 1, 3).reshape(2048, 128)
+
+
+def untiled(v):
+    return v.reshape(8, 32, 8, 128).transpose(0, 2, 1, 3).reshape(64, 4096)
+
+
+def vm(*shape, dtype=F32):
+    return pltpu.VMEM(shape, dtype)
+
+
+def shards(*args):
+    temp, base, store, level, face, area, rows, owner, tile = args
+    field = lambda: vm(64, 32, 128)
+    part = lambda: vm(48, 32, 128)
+    slot = lambda dtype=F32: vm(64, 128, dtype=dtype)
+    x, r, flag = pl.pallas_call(
+        step_kernel,
+        out_shape=[
+            jax.ShapeDtypeStruct((2048, 128), F32),
+            jax.ShapeDtypeStruct((2048, 128), F32),
+            jax.ShapeDtypeStruct((8, 128), F32),
+        ],
+        in_specs=[pl.BlockSpec(memory_space=pl.ANY)] * 9,
+        out_specs=[pl.BlockSpec(memory_space=pl.ANY)] * 2 + [pl.BlockSpec(memory_space=pltpu.VMEM)],
+        scratch_shapes=[
+            vm(2048, 128), vm(2048, 128), vm(2048, 128),
+            vm(32, 128, dtype=I32), vm(32, 128, dtype=I32), vm(32, 128), vm(256, 256),
+            vm(1, 256, dtype=I32), vm(1, 256, dtype=I32),
+            field(), field(), field(), part(), part(), part(),
+            field(), field(), field(), field(), field(), vm(2048, 128), vm(2048, 128),
+            vm(1024, 128, dtype=BF16), vm(32, 128, 256, dtype=BF16),
+            slot(I32), slot(I32), slot(I32), slot(I32), vm(32, 128, dtype=I32), vm(32, 128, dtype=I32),
+            slot(), slot(), vm(128, 128),
+            slot(), slot(), slot(), slot(), slot(), vm(256, 1024), vm(1024, 1024, dtype=BF16),
+            vm(ROUNDS, 128, 128), vm(ROUNDS, 128, 128), vm(128, 8, 256), vm(128, 8, 256),
+            pltpu.SemaphoreType.DMA((9,)),
+            pltpu.SemaphoreType.DMA((ROUNDS,)),
+            pltpu.SemaphoreType.DMA((ROUNDS,)),
+            pltpu.SemaphoreType.DMA,
+            pltpu.SemaphoreType.DMA,
+            pltpu.SemaphoreType.DMA((2,)),
+        ],
+        compiler_params=pltpu.CompilerParams(
+            collective_id=0, has_side_effects=True, vmem_limit_bytes=56 * 1024 * 1024
+        ),
+    )(
+        tiled(temp), tiled(base), tiled(store), level.reshape(32, 128),
+        face[0].T, area[0].T, rows[0], owner.reshape(1, 256), tile,
+    )
+    return lax.cond(
+        flag[0, 0] > 0.5,
+        lambda: general(*args),
+        lambda: (untiled(x), untiled(r)),
+    )
+
+
 def solution(mesh):
     return jax.shard_map(
         shards,

time: 1170 us -> 101 us (0.09)
  blocking collectives: 582 us -> 0 us
  local copies, waits for them, and re-layouts: 307 us -> 7.04 us
  other arithmetic: 192 us -> 0 us
  Pallas kernels: 0 us -> 92 us
  starting transfers between devices: 62.7 us -> 0 us
    psum x9 -> x0, blocking collectives: 582 us -> none  [the longest x5 318 us: squares(): return lax.psum(jnp.sum(values * values), ('bx', 'by'))]
    gather x7 -> x0, local copies, waits for them, and re-layouts: 139 us -> none  [the longest x4 92.1 us: apply_operator(): own_vals = values.reshape(-1)[voxel_lattice]]
    reshape x23 -> x0, local copies, waits for them, and re-layouts: 128 us -> none  [the longest x8 65.1 us: interface_energy_current(): flat_zero.at[voxel_lattice.reshape(-1)].add(flux_vals.reshape(-1))]
    scatter-add x5 -> x0, other arithmetic: 114 us -> none  [interface_energy_current(): flat_zero.at[voxel_lattice.reshape(-1)].add(flux_vals.reshape(-1))]
    pallas_call x0 -> x1, Pallas kernels: none -> 92 us  [shards(): pl.pallas_call(step_kernel, out_shape=[jax.ShapeDtypeStruct((2048, 128),...]
    all_to_all x8 -> x0, starting transfers between devices: 62.7 us -> none  [the longest x4 20.9 us: apply_operator(): lax.all_to_all(own_vals, ('bx', 'by'), split_axis=0, concat_axis=0, tiled...]
    mul x24 -> x0, other arithmetic: 24 us -> none  [the longest x5 8.01 us: inside_energy_current(): flux_one = interface_couplings[0] * (grid_cube[1:] - grid_cube[:-1])]
    reduce_sum x9 -> x0, other arithmetic: 22.7 us -> none  [the longest x4 13.8 us: squares(): return lax.psum(jnp.sum(values * values), ('bx', 'by'))]
  transfers between devices with their start and end apart: 8 -> 0, of which waited for: 4 -> 0; matrix products, arithmetic and copies ran while one was open for 19% -> 0% of each run, Pallas kernels for 0% -> 0%
where the time goes in v2:
time: 101 us
  Pallas kernels  92 us (91%)
  local copies, waits for them, and re-layouts  7.04 us (7%)
  between operations  1.56 us (2%)
    pallas_call x1, Pallas kernels, shards(): pl.pallas_call(step_kernel, out_shape=[jax.ShapeDtypeStruct((2048, 128),...  92 us
    unnamed x19, local copies, waits for them, and re-layouts  5.79 us

profile of v2, /device:TPU:1, one launch (start us, length us, event | category | flops | bytes accessed | tf_op | source)
XLA Modules:
  0.0 100.8 jit_solution(609222264496952530)
XLA Ops:
  0.6 0.0 copy-start.7
  0.6 0.0 copy-start.8
  0.7 0.0 copy-start.26
  0.7 0.0 copy-start.28
  0.7 2.4 %copy.90 = f32[64,4096]{1,0:T(8,128)} copy(f32[64,4096]{1,0:T(8,128)} %param.13) | data formatting | bytes 2097152
  3.1 0.0 copy-done.7
  3.1 0.0 copy-done.8
  3.1 0.0 copy-done.26
  3.1 0.0 copy-done.28
  3.1 92.0 %shard_map.108 = (f32[2048,128]{1,0:T(8,128)}, f32[2048,128]{1,0:T(8,128)}, f32[8,128]{1,0:T(8,128)}) custom-call(f32[2048,128]{1,0:T(8,128)} %bitcast.40.temp_hbm, f32[2048,128]{1,0:T(8,128)S(1)} %bitcast.126, f32[2048,128]{1,0:T(8,128)S(1)} %bitcast.127, s32[32,128]{1,0:T(8,128)} %bitcast.133, s32[32,128]{1,0:T(8,128)} %bitcast.134, f32[32,128]{1,0:T(8,128)} %bitcast.135, ...), custom_call_target="tpu_custom_call" | custom-call | tf_op jit(solution)/shard_map/pallas_call | solution.py:620
  95.1 0.0 copy-start.15
  95.2 0.0 copy-start.14
  95.2 0.0 copy-start.21
  95.2 0.0 copy-start.22
  95.2 2.4 %copy.91 = f32[2048,128]{1,0:T(8,128)} copy(f32[2048,128]{1,0:T(8,128)} %get-tuple-element.504) | data formatting | bytes 2097152
  97.5 0.0 copy-done.15
  97.5 1.0 copy.92
  98.5 1.2 %slice.87 = f32[1,1]{1,0:T(1,128)} slice(f32[8,128]{1,0:T(8,128)} %get-tuple-element.188), slice={[0:1], [0:1]} | slice | bytes 8 | tf_op jit(solution)/shard_map/slice | solution.py:655
  100.4 0.0 copy-done.14
  100.4 0.0 copy-done.21
  100.4 0.0 copy-done.22
  100.4 0.2 conditional.1
Async XLA Ops:
  0.6 2.5 %copy-start.7 = (f32[64,4096]{1,0:T(8,128)S(1)}, f32[64,4096]{1,0:T(8,128)}, u32[]{:S(2)}) copy-start(f32[64,4096]{1,0:T(8,128)} %param.14) | copy-start | bytes 3145732
  0.6 2.5 %copy-start.8 = (f32[64,4096]{1,0:T(8,128)S(1)}, f32[64,4096]{1,0:T(8,128)}, u32[]{:S(2)}) copy-start(f32[64,4096]{1,0:T(8,128)} %param.15) | copy-start | bytes 3145732
  0.7 2.5 %copy-start.26 = (s32[1,256,1]{1,2,0:T(1,128)S(1)}, s32[1,256,1]{1,2,0:T(1,128)}, u32[]{:S(2)}) copy-start(s32[1,256,1]{1,2,0:T(1,128)} %param.20) | copy-start | bytes 3076
  0.7 2.4 %copy-start.28 = (s32[1,256]{1,0:T(1,128)S(1)}, s32[1,256]{1,0:T(1,128)}, u32[]{:S(2)}) copy-start(s32[1,256]{1,0:T(1,128)} %tile_hbm.1) | copy-start | bytes 3076
  95.1 2.4 %copy-start.15 = (f32[2048,128]{1,0:T(8,128)S(1)}, f32[2048,128]{1,0:T(8,128)}, u32[]{:S(2)}) copy-start(f32[2048,128]{1,0:T(8,128)} %get-tuple-element.505) | copy-start | bytes 3145732
  95.2 5.3 %copy-start.14 = (f32[1,256,256]{2,1,0:T(8,128)S(1)}, f32[1,256,256]{2,1,0:T(8,128)}, u32[]{:S(2)}) copy-start(f32[1,256,256]{2,1,0:T(8,128)} %param.19) | copy-start | bytes 786436
  95.2 5.3 %copy-start.21 = (s32[4096]{0:T(1024)S(1)}, s32[4096]{0:T(1024)}, u32[]{:S(2)}) copy-start(s32[4096]{0:T(1024)} %param.16) | copy-start | bytes 49156
  95.2 5.3 %copy-start.22 = (s32[1,128,32]{1,2,0:T(8,128)S(1)}, s32[1,128,32]{1,2,0:T(8,128)}, u32[]{:S(2)}) copy-start(s32[1,128,32]{1,2,0:T(8,128)} %param.17) | copy-start | bytes 49156

commit v3 on v2

--- a/solution.py
+++ b/solution.py
@@ -12,6 +12,7 @@
 MESH = pl.DeviceIdType.MESH
 F32, BF16, I32 = jnp.float32, jnp.bfloat16, jnp.int32
 ROUNDS = 6
+MEMBERS = 5
 
 
 def cond_links(diffuse_warmth, spacing):
@@ -154,9 +155,8 @@
         return (conjugate_gradient_loop, equation_misfit, direction, next_norm)
 
     start_norm = squares(equation_misfit)
-    conjugate_gradient_loop, equation_misfit, direction, start_norm = lax.fori_loop(
-        0, ITERS, one_turn, (conjugate_gradient_loop, equation_misfit, equation_misfit, start_norm)
-    )
+    carry = one_turn(0, (conjugate_gradient_loop, equation_misfit, equation_misfit, start_norm))
+    conjugate_gradient_loop, equation_misfit, direction, start_norm = lax.fori_loop(1, ITERS, one_turn, carry)
     return (conjugate_gradient_loop, equation_misfit)
 
 
@@ -204,17 +204,29 @@
 
 def step_kernel(
     temp_hbm, base_hbm, store_hbm, level_hbm, face_hbm, area_hbm, rows_hbm, owner_hbm, tile_hbm,
-    x_out, r_out, flag_out,
+    x_out, r_out, p_out, w_out, s_out, flag_out, scale_out,
     in_t, in_b, in_s, level, face, area, rows, owner, tile,
     xf, kf, mf, gx, gy, gz, ra, rb, wf, sf, pf, nat, en,
     ohs, ohl, celltab, lanetab, srcrow, srclane, rowid, slane, slots, slots2, msgs,
-    ro, rp, so, sp, gface, heat, oht,
+    ro, wo, wp, zo, gface, heat, oht, uf, zf, kept, keys, members,
     snd, rcv, lsnd, lrcv,
     in_sem, ssem, rsem, lssem, lrsem, out_sem,
 ):
     bx, by = lax.axis_index("bx"), lax.axis_index("by")
     me = bx * 16 + by
     barrier = pltpu.get_barrier_semaphore()
+    def laser():
+        return pltpu.make_async_remote_copy(
+            src_ref=lsnd.at[pl.ds(0, 127)], dst_ref=lrcv.at[pl.ds(0, 127)],
+            send_sem=lssem, recv_sem=lrsem, device_id=(lax.rem(bx + 1, 8), by), device_id_type=MESH,
+        )
+
+    def all_of(r):
+        return pltpu.make_async_remote_copy(
+            src_ref=snd.at[r, pl.ds(0, 127)], dst_ref=rcv.at[r, pl.ds(0, 127)],
+            send_sem=ssem.at[r], recv_sem=rsem.at[r],
+            device_id=(lax.rem(bx + 1, 8), by), device_id_type=MESH,
+        )
     for px, py in peers():
         pl.semaphore_signal(barrier, inc=1, device_id=(px, py), device_id_type=MESH)
 
@@ -417,13 +429,6 @@
                 send_sem=ssem.at[r], recv_sem=rsem.at[r], device_id=(px, py), device_id_type=MESH,
             ).start()
 
-    def all_of(r):
-        return pltpu.make_async_remote_copy(
-            src_ref=snd.at[r, pl.ds(0, 127)], dst_ref=rcv.at[r, pl.ds(0, 127)],
-            send_sem=ssem.at[r], recv_sem=rsem.at[r],
-            device_id=(lax.rem(bx + 1, 8), by), device_id_type=MESH,
-        )
-
     def receive(r):
         all_of(r).wait_recv()
         return rcv[r].T
@@ -431,34 +436,92 @@
     def total(rows):
         return jnp.sum(rows, axis=1, keepdims=True)
 
+    def same_cell():
+        key = jnp.where(celltab[...] >= 0, celltab[...] * 128 + lanetab[...], -1)
+        keyt = key.astype(F32).T
+        most = jnp.zeros((1, 128), I32)
+        big = 1 << 20
+        kept[...] = keyt
+        keys[...] = key.astype(F32)
+
+        def one(b, most):
+            cols = []
+            for h in range(2):
+                hit = (iota((128, 64), 1) == b + 32 * h)
+                cols.append(jnp.sum(jnp.where(hit, kept[...], 0.0), axis=1, keepdims=True))
+            for h in range(2):
+                row = keys[pl.ds(b + 32 * h, 1), :]
+                cands = []
+                for g in range(2):
+                    same = jnp.logical_and(cols[g] == row, row >= 0.0)
+                    cands.append(jnp.where(same, iota((128, 128), 0) + 128 * g, big))
+                cand = jnp.concatenate(cands, axis=0)
+                for d in range(MEMBERS):
+                    low = jnp.min(cand, axis=0, keepdims=True)
+                    members[d, pl.ds(b + 32 * h, 1), :] = low
+                    cand = jnp.where(cand > low, cand, big)
+                most = jnp.maximum(most, (jnp.min(cand, axis=0, keepdims=True) < big).astype(I32))
+            return most
+
+        most = lax.fori_loop(0, 32, one, most)
+        return jnp.max(most.astype(F32), axis=1, keepdims=True)
+
+    def joined(f):
+        tops, lows = [], []
+        for g in range(4):
+            halves = [f[8 * g : 8 * g + 8, :], f[32 + 8 * g : 40 + 8 * g, :]]
+            for h, outs in ((0, tops), (1, lows)):
+                a = jnp.zeros((8, 128), F32)
+                for d in range(MEMBERS):
+                    m = members[d, pl.ds(32 * h + 8 * g, 8), :]
+                    at = m & 127
+                    v = jnp.where(m < 128, lanes_of(halves[0], at), lanes_of(halves[1], at))
+                    a = a + jnp.where(m < 256, v, 0.0)
+                outs.append(a)
+        return jnp.concatenate(tops + lows, axis=0)
+
+    def dot_all(v):
+        return jnp.sum(jnp.sum(v, axis=0, keepdims=True), axis=1, keepdims=True)
+
+    def spread(v):
+        return jnp.broadcast_to(v, (8, 128))
+
+    zero = jnp.zeros((8, 128), F32)
+    gather(kf, slots)
+    gather(xf, slots2)
+    round0 = [to_entries(slots), to_entries(slots2), ids]
     pl.semaphore_wait(barrier, 127)
     lrcv[pl.ds(me, 1)] = lsnd[pl.ds(me, 1)]
-
-    gather(kf, slots)
-    gather(xf, slots2)
-    send(0, [to_entries(slots), to_entries(slots2), ids, jnp.broadcast_to(over, (8, 128))])
-    for px, py in peers():
+    for n, (px, py) in enumerate(peers()):
+        if n == 48:
+            send(0, round0)
         pltpu.make_async_remote_copy(
             src_ref=lsnd.at[pl.ds(px * 16 + py, 1)], dst_ref=lrcv.at[pl.ds(me, 1)],
             send_sem=lssem, recv_sem=lrsem, device_id=(px, py), device_id_type=MESH,
         ).start()
+    many = same_cell()
     msgs[...] = receive(0)
     to_slots(msgs.at[pl.ds(0, 32)], gface)
-    to_slots(msgs.at[pl.ds(32, 32)], rp)
-    to_slots(area, ro)
-    gface[...] = ro[...] * 0.5 * (slots[...] + gface[...])
-    slots[...] = gface[...] * (slots2[...] - rp[...])
+    to_slots(msgs.at[pl.ds(32, 32)], wp)
+    to_slots(area, wo)
+    gface[...] = wo[...] * 0.5 * (slots[...] + gface[...])
+    slots[...] = gface[...] * (slots2[...] - wp[...])
     scatter(slots)
-    flag_out[...] = jnp.broadcast_to(jnp.max(msgs[72:80, :], axis=1, keepdims=True), (8, 128))
     tids = msgs[64:72, :].astype(I32)
     for j in range(8):
         oht[:, pl.ds(128 * j, 128)] = (iota((1024, 128), 0) == tids[j : j + 1]).astype(F32).astype(BF16)
 
-    laser = pltpu.make_async_remote_copy(
-        src_ref=lsnd.at[pl.ds(0, 127)], dst_ref=lrcv.at[pl.ds(0, 127)],
-        send_sem=lssem, recv_sem=lrsem, device_id=(lax.rem(bx + 1, 8), by), device_id_type=MESH,
-    )
-    laser.wait_recv()
+    def first(k, c):
+        at = pl.ds(8 * k, 8)
+
+        def emit(c, a):
+            rb[c, at, :] = a + nat[pl.ds(512 * k + c, 8, stride=64), :]
+
+        stencil(k, lambda c: xf[c, at, :], emit, False)
+        return c
+
+    lax.fori_loop(0, 4, first, 0)
+    laser().wait_recv()
     by_rank = []
     for j in range(8):
         by_rank.append(lrcv[:, j, :])
@@ -466,138 +529,173 @@
     for q in range(8):
         o = oht[pl.ds(128 * q, 128), :]
         h = (dot_nn(o, pieces[0]) + dot_nn(o, pieces[1])) + dot_nn(o, pieces[2])
-        heat[:, pl.ds(128 * q, 128)] = h.T
-    lane = iota((8, 128), 1)
-    for b in range(32):
-        idx = 32 * (b % 4) + (lane >> 2)
-        for g in range(8):
-            a = jnp.zeros((8, 128), F32)
-            for q in range(4):
-                v = heat[64 * q + 8 * g : 64 * q + 8 * g + 8, 128 * (b // 4) : 128 * (b // 4) + 128]
-                a = jnp.where((lane & 3) == q, lanes_of(v, idx), a)
-            en[64 * b + 8 * g : 64 * b + 8 * g + 8, :] = a
-
-    def first(k, rr):
+        for part in range(4):
+            heat[pl.ds(512 * q + part, 128, stride=4), :] = h[:, 64 * part : 64 * part + 64]
+        for b in range(4 * q, 4 * q + 4):
+            en[64 * b : 64 * b + 64, :] = heat[128 * b : 128 * b + 128, :].T
+
+    def start(k, c):
         at = pl.ds(8 * k, 8)
-        total_rr = [rr]
+        for c in range(64):
+            ra[c, at, :] = en[pl.ds(512 * k + c, 8, stride=64), :] - rb[c, at, :]
+        return 0
+
+    lax.fori_loop(0, 4, start, 0)
+    gather(ra, ro)
+    send(1, [to_entries(ro), spread(jnp.maximum(over, many))])
+
+    def early(k, sums):
+        at = pl.ds(8 * k, 8)
+        s = list(sums)
 
         def emit(c, a):
-            here = pl.ds(512 * k + c, 8, stride=64)
-            r = en[here, :] - (a + nat[here, :])
-            ra[c, at, :] = r
-            total_rr[0] = total_rr[0] + r * r
-
-        stencil(k, lambda c: xf[c, at, :], emit, False)
-        return total_rr[0]
-
-    zero = jnp.zeros((8, 128), F32)
-    lax.fori_loop(0, 4, first, zero)
-    gather(ra, ro)
-    send(1, [to_entries(ro)])
+            r = ra[c, at, :]
+            wf[c, at, :] = a
+            s[0] = s[0] + r * r
+            s[1] = s[1] + r * a
+
+        stencil(k, lambda c: ra[c, at, :], emit, True)
+        return tuple(s)
+
+    rr, rw = [dot_all(v) for v in lax.fori_loop(0, 4, early, (zero, zero))]
+    gather(wf, wo)
     msgs[...] = receive(1)
-    to_slots(msgs.at[pl.ds(0, 32)], rp)
-
-    def image(rnew, load):
-        slots[...] = gface[...] * (ro[...] - rp[...])
-        scatter(slots)
-
-        def group(k, sums):
-            at = pl.ds(8 * k, 8)
-            s = list(sums)
-
-            def emit(c, a):
-                r = rnew[c, at, :]
-                w = a + nat[pl.ds(512 * k + c, 8, stride=64), :]
-                wf[c, at, :] = w
-                s[0] = s[0] + r * r
-                s[1] = s[1] + r * w
-
-            stencil(k, lambda c: load(k, c), emit, True)
-            return tuple(s)
-
-        rr, rw = lax.fori_loop(0, 4, group, (zero, zero))
-        full = [jnp.sum(jnp.sum(v, axis=0, keepdims=True), axis=1, keepdims=True) for v in (rr, rw)]
-        return [jnp.broadcast_to(v, (8, 128)) for v in full]
-
-    rr, rw = image(ra, lambda k, c: ra[c, pl.ds(8 * k, 8), :])
-    old_rr = old_alpha = None
+    flag_out[...] = spread(jnp.max(msgs[32:40, :], axis=1, keepdims=True))
+    to_slots(msgs.at[pl.ds(0, 32)], wp)
+    flux = gface[...] * (ro[...] - wp[...])
+    slots[...] = flux
+    rw = rw + dot_all(ro[...] * flux)
+    wo[...] = wo[...] + joined(flux)
+
+    old_rr = old_alpha = alpha1 = beta1 = None
     r_now, r_next = ra, rb
     for it in range(ITERS):
         last = it == ITERS - 1
         if last:
-            send(it + 2, [rr, rw])
+            send(it + 2, [spread(rr), spread(rw)])
         else:
-            gather(wf, slots)
-            send(it + 2, [to_entries(slots), rr, rw])
+            send(it + 2, [to_entries(wo), spread(rr), spread(rw)])
+        scatter(slots)
         if it:
-            def advance(k, c, it=it, beta=beta, alpha=alpha, r_old=r_old):
-                at = pl.ds(8 * k, 8)
-                for cell in range(64):
-                    d = r_old[cell, at, :]
-                    if it > 1:
-                        d = d + beta * pf[cell, at, :]
-                    pf[cell, at, :] = d
-                    xf[cell, at, :] = xf[cell, at, :] + alpha * d
-                return c
-
-            lax.fori_loop(0, 4, advance, 0)
+            r_now, r_next = r_next, r_now
+            alpha, beta = spread(alpha1), None if it == 1 else spread(beta1)
+
+        def along(k, sums, it=it, last=last, r_now=r_now, r_next=r_next):
+            at = pl.ds(8 * k, 8)
+            d = list(sums)
+
+            def load(c):
+                here = nat[pl.ds(512 * k + c, 8, stride=64), :]
+                if it == 0:
+                    w = wf[c, at, :] + here
+                    wf[c, at, :] = w
+                    d[2] = d[2] + w * w
+                    return w
+                w = wf[c, at, :]
+                z = uf[c, at, :] + here
+                s = w
+                r = r_next[c, at, :]
+                q = r
+                if it > 1:
+                    z = z + beta * zf[c, at, :]
+                    s = s + beta * sf[c, at, :]
+                    q = q + beta * pf[c, at, :]
+                pf[c, at, :] = q
+                xf[c, at, :] = xf[c, at, :] + alpha * q
+                sf[c, at, :] = s
+                r = r - alpha * s
+                w = w - alpha * z
+                r_now[c, at, :] = r
+                wf[c, at, :] = w
+                if not last:
+                    zf[c, at, :] = z
+                    for n, (p, q) in enumerate(((r, r), (r, w), (w, w), (r, s), (w, s), (s, s), (w, z), (s, z))):
+                        d[n] = d[n] + p * q
+                return w
+
+            def emit(c, a):
+                uf[c, at, :] = a
+                d[8] = d[8] + wf[c, at, :] * a
+
+            if last:
+                for c in range(64):
+                    load(c)
+            else:
+                stencil(k, load, emit, True)
+            return tuple(d)
+
+        dots = lax.fori_loop(0, 4, along, (zero,) * 9)
+        if last:
+            outs = [
+                pltpu.make_async_copy(src, dst, out_sem.at[n])
+                for n, (src, dst) in enumerate(zip((xf, r_now, pf, wf, sf), (x_out, r_out, p_out, w_out, s_out)))
+            ]
+            for c in outs:
+                c.start()
+        else:
+            dots = [dot_all(v) for v in dots]
+            if it == 0:
+                dots[0], dots[1] = rr, rw
+            gather(uf, slots2)
         msgs[...] = receive(it + 2)
         base = 0 if last else 32
         g_rr, g_rw = total(msgs[base : base + 1, :]), total(msgs[base + 8 : base + 9, :])
         if it:
             beta1 = g_rr / old_rr
             alpha1 = g_rr / (g_rw - beta1 * g_rr / old_alpha)
-            beta = jnp.broadcast_to(beta1, (8, 128))
         else:
             alpha1 = g_rr / g_rw
-            beta = None
-        alpha = jnp.broadcast_to(alpha1, (8, 128))
         old_rr, old_alpha = g_rr, alpha1
-        r_old = r_now
         if last:
             break
-        to_slots(msgs.at[pl.ds(0, 32)], slots2)
+        to_slots(msgs.at[pl.ds(0, 32)], wp)
+        flux = gface[...] * (wo[...] - wp[...])
+        slots[...] = flux
+        rr, rw, ww, rs, ws, ss, wz, sz, wu = dots
+        wq = wu + dot_all(wo[...] * flux)
+        z = slots2[...] + joined(flux)
+        s = wo[...]
         if it:
-            so[...] = slots[...] + beta1 * so[...]
-            sp[...] = slots2[...] + beta1 * sp[...]
+            z = z + beta1 * zo[...]
+            rs = rw + beta1 * rs
+            ss = ww + beta1 * (2.0 * ws + beta1 * ss)
+            sz = wq + beta1 * (2.0 * wz + beta1 * sz)
+            ws = ww + beta1 * ws
         else:
-            so[...] = slots[...]
-            sp[...] = slots2[...]
-        ro[...] = ro[...] - alpha1 * so[...]
-        rp[...] = rp[...] - alpha1 * sp[...]
-
-        def load(k, c, it=it, alpha=alpha, beta=beta, r_now=r_now, r_next=r_next):
-            at = pl.ds(8 * k, 8)
-            s = wf[c, at, :]
-            if it:
-                s = s + beta * sf[c, at, :]
-            sf[c, at, :] = s
-            r = r_now[c, at, :] - alpha * s
-            r_next[c, at, :] = r
-            return r
-
-        rr, rw = image(r_next, load)
-        r_now, r_next = r_next, r_now
-
-    def finish(k, c):
-        at = pl.ds(8 * k, 8)
-        for cell in range(64):
-            where = pl.ds((cell // 8) * 256 + cell % 8 + 64 * k, 8, stride=8)
-            r = r_now[cell, at, :]
-            d = r + beta * pf[cell, at, :]
-            in_t[where, :] = xf[cell, at, :] + alpha * d
-            in_b[where, :] = r - alpha * (wf[cell, at, :] + beta * sf[cell, at, :])
-        return c
-
-    lax.fori_loop(0, 4, finish, 0)
-    outs = [pltpu.make_async_copy(in_t, x_out, out_sem.at[0]), pltpu.make_async_copy(in_b, r_out, out_sem.at[1])]
-    for c in outs:
-        c.start()
+            rs, ss, sz, ws = rw, ww, wq, ww
+        zo[...] = z
+        wo[...] = s - alpha1 * z
+        rr = rr + alpha1 * (alpha1 * ss - 2.0 * rs)
+        rw = rw + alpha1 * (alpha1 * sz - 2.0 * ws)
+
+    scale_out[0:8, :] = spread(alpha1)
+    scale_out[8:16, :] = spread(beta1)
     for r in range(ROUNDS):
         all_of(r).wait_send()
-    laser.wait_send()
+    laser().wait_send()
     for c in outs:
         c.wait()
+
+
+def finish_kernel(scale, x, r, p, w, s, x_out, r_out):
+    alpha, beta = scale[0:8, :], scale[8:16, :]
+    for c in range(64):
+        to = pl.ds(c % 8, 8, stride=8)
+        x_out[c // 8, to, :] = x[c] + alpha * (r[c] + beta * p[c])
+        r_out[c // 8, to, :] = r[c] - alpha * (w[c] + beta * s[c])
+
+
+def finish(scale, *fields):
+    of = pl.BlockSpec((64, 8, 128), lambda k: (0, k, 0))
+    to = pl.BlockSpec((8, 64, 128), lambda k: (0, k, 0))
+    x, r = pl.pallas_call(
+        finish_kernel,
+        grid=(4,),
+        out_shape=[jax.ShapeDtypeStruct((8, 256, 128), F32)] * 2,
+        in_specs=[pl.BlockSpec((16, 128), lambda k: (0, 0))] + [of] * 5,
+        out_specs=[to] * 2,
+    )(scale, *fields)
+    return untiled(x), untiled(r)
 
 
 def tiled(v):
@@ -617,15 +715,15 @@
     field = lambda: vm(64, 32, 128)
     part = lambda: vm(48, 32, 128)
     slot = lambda dtype=F32: vm(64, 128, dtype=dtype)
-    x, r, flag = pl.pallas_call(
+    *fields, flag, scale = pl.pallas_call(
         step_kernel,
         out_shape=[
-            jax.ShapeDtypeStruct((2048, 128), F32),
-            jax.ShapeDtypeStruct((2048, 128), F32),
+            *[jax.ShapeDtypeStruct((64, 32, 128), F32)] * 5,
             jax.ShapeDtypeStruct((8, 128), F32),
+            jax.ShapeDtypeStruct((16, 128), F32),
         ],
         in_specs=[pl.BlockSpec(memory_space=pl.ANY)] * 9,
-        out_specs=[pl.BlockSpec(memory_space=pl.ANY)] * 2 + [pl.BlockSpec(memory_space=pltpu.VMEM)],
+        out_specs=[pl.BlockSpec(memory_space=pl.ANY)] * 5 + [pl.BlockSpec(memory_space=pltpu.VMEM)] * 2,
         scratch_shapes=[
             vm(2048, 128), vm(2048, 128), vm(2048, 128),
             vm(32, 128, dtype=I32), vm(32, 128, dtype=I32), vm(32, 128), vm(256, 256),
@@ -635,17 +733,18 @@
             vm(1024, 128, dtype=BF16), vm(32, 128, 256, dtype=BF16),
             slot(I32), slot(I32), slot(I32), slot(I32), vm(32, 128, dtype=I32), vm(32, 128, dtype=I32),
             slot(), slot(), vm(128, 128),
-            slot(), slot(), slot(), slot(), slot(), vm(256, 1024), vm(1024, 1024, dtype=BF16),
+            slot(), slot(), slot(), slot(), slot(), vm(4096, 64), vm(1024, 1024, dtype=BF16),
+            field(), field(), vm(128, 64), slot(), vm(MEMBERS, 64, 128, dtype=I32),
             vm(ROUNDS, 128, 128), vm(ROUNDS, 128, 128), vm(128, 8, 256), vm(128, 8, 256),
             pltpu.SemaphoreType.DMA((9,)),
             pltpu.SemaphoreType.DMA((ROUNDS,)),
             pltpu.SemaphoreType.DMA((ROUNDS,)),
             pltpu.SemaphoreType.DMA,
             pltpu.SemaphoreType.DMA,
-            pltpu.SemaphoreType.DMA((2,)),
+            pltpu.SemaphoreType.DMA((5,)),
         ],
         compiler_params=pltpu.CompilerParams(
-            collective_id=0, has_side_effects=True, vmem_limit_bytes=56 * 1024 * 1024
+            collective_id=0, has_side_effects=True, vmem_limit_bytes=63 * 1024 * 1024
         ),
     )(
         tiled(temp), tiled(base), tiled(store), level.reshape(32, 128),
@@ -654,7 +753,7 @@
     return lax.cond(
         flag[0, 0] > 0.5,
         lambda: general(*args),
-        lambda: (untiled(x), untiled(r)),
+        lambda: finish(scale, *fields),
     )
 
 

time: 101 us -> 83 us (0.82)
  Pallas kernels: 92 us -> 80.2 us
  local copies, waits for them, and re-layouts: 7.04 us -> 1.21 us
    pallas_call x1 -> x2, Pallas kernels: 92 us -> 80.2 us  [the longest x1 75.7 us: shards(): pl.pallas_call(step_kernel, out_shape=[*[jax.ShapeDtypeStruct((64, 32, 12...]
    unnamed x19 -> x6, local copies, waits for them, and re-layouts: 5.79 us -> 0.01 us
where the time goes in v3:
time: 83 us; the launch traced here: 82.7 us
  Pallas kernels  80.2 us (97%)
  between operations  1.34 us (2%)
  local copies, waits for them, and re-layouts  1.21 us (1%)
    pallas_call x1, Pallas kernels, shards(): pl.pallas_call(step_kernel, out_shape=[*[jax.ShapeDtypeStruct((64, 32, 12...  75.7 us
    pallas_call x1, Pallas kernels, finish(): pl.pallas_call(finish_kernel, grid=(4,), out_shape=[jax.ShapeDtypeStruct(...  4.46 us

profile of v3, /device:TPU:1, one launch (start us, length us, event | category | flops | bytes accessed | tf_op | source)
XLA Modules:
  0.0 82.7 jit_solution(4222746683357509151)
XLA Ops:
  0.6 0.0 copy-start.34
  0.6 0.0 copy-start.24
  0.7 0.0 copy-start.38
  0.7 75.7 %shard_map.108 = (f32[64,32,128]{2,1,0:T(8,128)}, f32[64,32,128]{2,1,0:T(8,128)}, f32[64,32,128]{2,1,0:T(8,128)}, f32[64,32,128]{2,1,0:T(8,128)}, f32[64,32,128]...) custom-call(f32[2048,128]{1,0:T(8,128)} %bitcast.124, f32[2048,128]{1,0:T(8,128)} %bitcast.131, ...), custom_call_target="tpu_custom_call" | custom-call | tf_op jit(solution)/shard_map/pallas_call | solution.py:718
  76.4 1.2 %slice.107 = f32[1,1]{1,0:T(1,128)} slice(f32[8,128]{1,0:T(8,128)} %get-tuple-element.206), slice={[0:1], [0:1]} | slice | bytes 8 | tf_op jit(solution)/shard_map/slice | solution.py:754
  78.2 0.0 copy-done.34
  78.2 0.0 copy-done.24
  78.2 0.0 copy-done.38
  78.3 4.5 %conditional.1 = (f32[64,4096]{1,0:T(8,128)}, f32[64,4096]{1,0:T(8,128)}) conditional(s32[]{:T(128)} %bitcast.55, (f32[16,128]{1,0:T(8,128)S(1)}, f32[64,32,128]{2,1,0:T(8,128)}, f32[64,32,128]{2,1,0:T(8,128)}, f32[64,32,128]{2,1,0:T(8,128)}, f32[64,32,128]{2,1,0:T(8,128)}, /*index=5*/f32[64,32,128]{2,1,0:T(8,128)}) %tuple.27, ...), branch_computations={%region_0.0_spmd, %region_1.22_spmd} | conditional | flops 3247519744 | bytes 288816960 | solution.py:753
  78.3 4.5 %branch_0_fun.1 = (f32[8,256,128]{2,1,0:T(8,128)}, f32[8,256,128]{2,1,0:T(8,128)}) custom-call(f32[16,128]{1,0:T(8,128)S(1)} %get-tuple-element.165.scale, f32[64,32,128]{2,1,0:T(8,128)} %get-tuple-element.166.x, f32[64,32,128]{2,1,0:T(8,128)} %get-tuple-element.167.r, f32[64,32,128]{2,1,0:T(8,128)} %get-tuple-element.168.p, ...), custom_call_target="tpu_custom_call" | custom-call | tf_op jit(solution)/shard_map/cond/branch_0_fun/pallas_call | solution.py:691
Async XLA Ops:
  0.6 77.6 %copy-start.34 = (s32[4096]{0:T(1024)S(1)}, s32[4096]{0:T(1024)}, u32[]{:S(2)}) copy-start(s32[4096]{0:T(1024)} %param.16) | copy-start | bytes 49156
  0.6 77.6 %copy-start.24 = (f32[1,256,256]{2,1,0:T(8,128)S(1)}, f32[1,256,256]{2,1,0:T(8,128)}, u32[]{:S(2)}) copy-start(f32[1,256,256]{2,1,0:T(8,128)} %param.19) | copy-start | bytes 786436
  0.7 77.6 %copy-start.38 = (s32[1,256,1]{1,2,0:T(1,128)S(1)}, s32[1,256,1]{1,2,0:T(1,128)}, u32[]{:S(2)}) copy-start(s32[1,256,1]{1,2,0:T(1,128)} %param.20) | copy-start | bytes 3076

commit v4 on v3

--- a/solution.py
+++ b/solution.py
@@ -12,7 +12,6 @@
 MESH = pl.DeviceIdType.MESH
 F32, BF16, I32 = jnp.float32, jnp.bfloat16, jnp.int32
 ROUNDS = 6
-MEMBERS = 5
 
 
 def cond_links(diffuse_warmth, spacing):
@@ -196,10 +195,13 @@
                         offs.append((-hops, dc, dy, dx, dz))
     offs.sort()
     y, core, x, z = bx // 2, lax.rem(bx, 2), by // 4, lax.rem(by, 4)
-    for _, dc, dy, dx, dz in offs:
-        px = lax.rem(y + dy, 4) * 2 + lax.rem(core + dc, 2)
-        py = lax.rem(x + dx, 4) * 4 + lax.rem(z + dz, 4)
-        yield px, py
+    ys = [lax.rem(y + d, 4) * 2 for d in range(4)]
+    cores = [lax.rem(core + d, 2) for d in range(2)]
+    xs = [lax.rem(x + d, 4) * 4 for d in range(4)]
+    zs = [lax.rem(z + d, 4) for d in range(4)]
+    pxs = [[ys[d] + cores[e] for e in range(2)] for d in range(4)]
+    pys = [[xs[d] + zs[e] for e in range(4)] for d in range(4)]
+    return [(pxs[dy][dc], pys[dx][dz], pxs[dy][dc] * 16 + pys[dx][dz]) for _, dc, dy, dx, dz in offs]
 
 
 def step_kernel(
@@ -208,7 +210,7 @@
     in_t, in_b, in_s, level, face, area, rows, owner, tile,
     xf, kf, mf, gx, gy, gz, ra, rb, wf, sf, pf, nat, en,
     ohs, ohl, celltab, lanetab, srcrow, srclane, rowid, slane, slots, slots2, msgs,
-    ro, wo, wp, zo, gface, heat, oht, uf, zf, kept, keys, members,
+    ro, wo, zo, gface, flows, heat, oht, uf, zf, kept, keys, place_of, list_row, list_lane, mates,
     snd, rcv, lsnd, lrcv,
     in_sem, ssem, rsem, lssem, lrsem, out_sem,
 ):
@@ -227,7 +229,8 @@
             send_sem=ssem.at[r], recv_sem=rsem.at[r],
             device_id=(lax.rem(bx + 1, 8), by), device_id_type=MESH,
         )
-    for px, py in peers():
+    others = peers()
+    for px, py, _ in others:
         pl.semaphore_signal(barrier, inc=1, device_id=(px, py), device_id_type=MESH)
 
     loads = [
@@ -395,7 +398,7 @@
             nat[pl.ds(64 * b, 64), :] = (o[0:64] + o[64:128]) + o[128:192]
             return c
 
-        lax.fori_loop(0, 32, one, 0, unroll=4)
+        lax.fori_loop(0, 32, one, 0, unroll=16)
 
     def stencil(k, load, emit, mass):
         at = pl.ds(8 * k, 8)
@@ -423,9 +426,9 @@
         full = jnp.concatenate(list(feats) + [jnp.zeros((128 - n, 128), F32)], axis=0)
         snd[r] = full.T
         rcv[r, pl.ds(me, 1), :] = snd[r, pl.ds(me, 1), :]
-        for px, py in peers():
+        for px, py, p in others:
             pltpu.make_async_remote_copy(
-                src_ref=snd.at[r, pl.ds(px * 16 + py, 1)], dst_ref=rcv.at[r, pl.ds(me, 1)],
+                src_ref=snd.at[r, pl.ds(p, 1)], dst_ref=rcv.at[r, pl.ds(me, 1)],
                 send_sem=ssem.at[r], recv_sem=rsem.at[r], device_id=(px, py), device_id_type=MESH,
             ).start()
 
@@ -437,48 +440,64 @@
         return jnp.sum(rows, axis=1, keepdims=True)
 
     def same_cell():
-        key = jnp.where(celltab[...] >= 0, celltab[...] * 128 + lanetab[...], -1)
-        keyt = key.astype(F32).T
-        most = jnp.zeros((1, 128), I32)
-        big = 1 << 20
-        kept[...] = keyt
-        keys[...] = key.astype(F32)
-
-        def one(b, most):
+        key = jnp.where(celltab[...] >= 0, celltab[...] * 128 + lanetab[...], -1).astype(F32)
+        kept[...] = key.T
+        keys[...] = key
+
+        def one(b, c):
             cols = []
             for h in range(2):
-                hit = (iota((128, 64), 1) == b + 32 * h)
+                hit = iota((128, 64), 1) == b + 32 * h
                 cols.append(jnp.sum(jnp.where(hit, kept[...], 0.0), axis=1, keepdims=True))
             for h in range(2):
                 row = keys[pl.ds(b + 32 * h, 1), :]
-                cands = []
+                n = jnp.zeros((1, 128), F32)
                 for g in range(2):
-                    same = jnp.logical_and(cols[g] == row, row >= 0.0)
-                    cands.append(jnp.where(same, iota((128, 128), 0) + 128 * g, big))
-                cand = jnp.concatenate(cands, axis=0)
-                for d in range(MEMBERS):
-                    low = jnp.min(cand, axis=0, keepdims=True)
-                    members[d, pl.ds(b + 32 * h, 1), :] = low
-                    cand = jnp.where(cand > low, cand, big)
-                most = jnp.maximum(most, (jnp.min(cand, axis=0, keepdims=True) < big).astype(I32))
-            return most
-
-        most = lax.fori_loop(0, 32, one, most)
-        return jnp.max(most.astype(F32), axis=1, keepdims=True)
+                    n = n + jnp.sum(jnp.where(cols[g] == row, 1.0, 0.0), axis=0, keepdims=True)
+                slots2[pl.ds(b + 32 * h, 1), :] = jnp.where(n > 1.5, 1.0, 0.0)
+            return c
+
+        lax.fori_loop(0, 32, one, 0)
+        shared = to_entries(slots2).astype(BF16)
+        rows_before = dot_nn((iota((32, 32), 1) < iota((32, 32), 0)).astype(F32).astype(BF16), shared)
+        at = dot_nn(shared, tri) + dot_nn(rows_before.astype(BF16), ones) - 1.0
+        at = jnp.where(shared.astype(F32) > 0.5, at, -1.0)
+        most = jnp.max(jnp.max(at, axis=0, keepdims=True), axis=1, keepdims=True)
+        at = at.astype(I32)
+        place_of[...] = at
+        acc = jnp.zeros((16, 128), F32)
+        for i in range(32):
+            hit = (iota((128, 128), 0) == at[i : i + 1]).astype(F32).astype(BF16)
+            row = fc[i : i + 1]
+            vals = [jnp.full((1, 128), i + 1, I32), iota((1, 128), 1), row >> 12, (row >> 7) & 31, row & 127]
+            vals = jnp.concatenate(vals + [jnp.zeros((11, 128), I32)], axis=0)
+            acc = acc + dot_nt(vals.astype(F32).astype(BF16), hit)
+        list_row[...] = jnp.broadcast_to(acc[0:1].astype(I32) - 1, (8, 128))
+        list_lane[...] = jnp.broadcast_to(acc[1:2].astype(I32), (8, 128))
+        name = acc[2:3] * 4096.0 + acc[3:4] * 128.0 + acc[4:5]
+        name = jnp.broadcast_to(jnp.where(acc[0:1] > 0.5, name, -1.0), (128, 128))
+        other = iota((128, 128), 0) != iota((128, 128), 1)
+        same = jnp.logical_and(jnp.logical_and(name == name.T, name >= 0.0), other)
+        mates[...] = jnp.where(same, 1.0, 0.0).astype(BF16)
+        return jnp.where(most > 127.5, 1.0, 0.0)
 
     def joined(f):
-        tops, lows = [], []
+        got = jnp.zeros((8, 128), F32)
         for g in range(4):
-            halves = [f[8 * g : 8 * g + 8, :], f[32 + 8 * g : 40 + 8 * g, :]]
-            for h, outs in ((0, tops), (1, lows)):
-                a = jnp.zeros((8, 128), F32)
-                for d in range(MEMBERS):
-                    m = members[d, pl.ds(32 * h + 8 * g, 8), :]
-                    at = m & 127
-                    v = jnp.where(m < 128, lanes_of(halves[0], at), lanes_of(halves[1], at))
-                    a = a + jnp.where(m < 256, v, 0.0)
-                outs.append(a)
-        return jnp.concatenate(tops + lows, axis=0)
+            v = lanes_of(f[8 * g : 8 * g + 8, :], list_lane[...])
+            got = got + jnp.where(list_row[...] == iota((8, 128), 0) + 8 * g, v, 0.0)
+        got = jnp.sum(got, axis=0, keepdims=True)
+        p0 = got.astype(BF16).astype(F32)
+        p1 = (got - p0).astype(BF16).astype(F32)
+        p = jnp.concatenate([p0, p1, got - p0 - p1, jnp.zeros((13, 128), F32)], axis=0).astype(BF16)
+        o = dot_nn(p, mates[...])
+        more = jnp.broadcast_to((o[0:1] + o[1:2]) + o[2:3], (8, 128))
+        outs = []
+        for g in range(4):
+            at = place_of[8 * g : 8 * g + 8, :]
+            v = lanes_of(more, jnp.maximum(at, 0) & 127)
+            outs.append(f[8 * g : 8 * g + 8, :] + jnp.where(at >= 0, v, 0.0))
+        return jnp.concatenate(outs, axis=0)
 
     def dot_all(v):
         return jnp.sum(jnp.sum(v, axis=0, keepdims=True), axis=1, keepdims=True)
@@ -489,23 +508,24 @@
     zero = jnp.zeros((8, 128), F32)
     gather(kf, slots)
     gather(xf, slots2)
-    round0 = [to_entries(slots), to_entries(slots2), ids]
+    k_own, t_own = to_entries(slots), to_entries(slots2)
+    wo[...] = k_own
+    zo[...] = t_own
+    round0 = [k_own, t_own, ids]
     pl.semaphore_wait(barrier, 127)
     lrcv[pl.ds(me, 1)] = lsnd[pl.ds(me, 1)]
-    for n, (px, py) in enumerate(peers()):
+    for n, (px, py, p) in enumerate(others):
         if n == 48:
             send(0, round0)
         pltpu.make_async_remote_copy(
-            src_ref=lsnd.at[pl.ds(px * 16 + py, 1)], dst_ref=lrcv.at[pl.ds(me, 1)],
+            src_ref=lsnd.at[pl.ds(p, 1)], dst_ref=lrcv.at[pl.ds(me, 1)],
             send_sem=lssem, recv_sem=lrsem, device_id=(px, py), device_id_type=MESH,
         ).start()
     many = same_cell()
     msgs[...] = receive(0)
-    to_slots(msgs.at[pl.ds(0, 32)], gface)
-    to_slots(msgs.at[pl.ds(32, 32)], wp)
-    to_slots(area, wo)
-    gface[...] = wo[...] * 0.5 * (slots[...] + gface[...])
-    slots[...] = gface[...] * (slots2[...] - wp[...])
+    gface[...] = area[...] * 0.5 * (wo[...] + msgs[0:32, :])
+    flows[...] = gface[...] * (zo[...] - msgs[32:64, :])
+    to_slots(flows, slots)
     scatter(slots)
     tids = msgs[64:72, :].astype(I32)
     for j in range(8):
@@ -541,8 +561,9 @@
         return 0
 
     lax.fori_loop(0, 4, start, 0)
-    gather(ra, ro)
-    send(1, [to_entries(ro), spread(jnp.maximum(over, many))])
+    gather(ra, slots2)
+    ro[...] = to_entries(slots2)
+    send(1, [ro[...], spread(jnp.maximum(over, many))])
 
     def early(k, sums):
         at = pl.ds(8 * k, 8)
@@ -558,12 +579,12 @@
         return tuple(s)
 
     rr, rw = [dot_all(v) for v in lax.fori_loop(0, 4, early, (zero, zero))]
-    gather(wf, wo)
+    gather(wf, slots2)
+    wo[...] = to_entries(slots2)
     msgs[...] = receive(1)
-    flag_out[...] = spread(jnp.max(msgs[32:40, :], axis=1, keepdims=True))
-    to_slots(msgs.at[pl.ds(0, 32)], wp)
-    flux = gface[...] * (ro[...] - wp[...])
-    slots[...] = flux
+    flag_out[...] = jnp.max(msgs[32:33, :], axis=1, keepdims=True)
+    flux = gface[...] * (ro[...] - msgs[0:32, :])
+    flows[...] = flux
     rw = rw + dot_all(ro[...] * flux)
     wo[...] = wo[...] + joined(flux)
 
@@ -574,7 +595,8 @@
         if last:
             send(it + 2, [spread(rr), spread(rw)])
         else:
-            send(it + 2, [to_entries(wo), spread(rr), spread(rw)])
+            send(it + 2, [wo[...], spread(rr), spread(rw)])
+        to_slots(flows, slots)
         scatter(slots)
         if it:
             r_now, r_next = r_next, r_now
@@ -637,6 +659,7 @@
             if it == 0:
                 dots[0], dots[1] = rr, rw
             gather(uf, slots2)
+            ro[...] = to_entries(slots2)
         msgs[...] = receive(it + 2)
         base = 0 if last else 32
         g_rr, g_rw = total(msgs[base : base + 1, :]), total(msgs[base + 8 : base + 9, :])
@@ -648,12 +671,11 @@
         old_rr, old_alpha = g_rr, alpha1
         if last:
             break
-        to_slots(msgs.at[pl.ds(0, 32)], wp)
-        flux = gface[...] * (wo[...] - wp[...])
-        slots[...] = flux
+        flux = gface[...] * (wo[...] - msgs[0:32, :])
+        flows[...] = flux
         rr, rw, ww, rs, ws, ss, wz, sz, wu = dots
         wq = wu + dot_all(wo[...] * flux)
-        z = slots2[...] + joined(flux)
+        z = ro[...] + joined(flux)
         s = wo[...]
         if it:
             z = z + beta1 * zo[...]
@@ -679,15 +701,16 @@
 
 def finish_kernel(scale, x, r, p, w, s, x_out, r_out):
     alpha, beta = scale[0:8, :], scale[8:16, :]
-    for c in range(64):
-        to = pl.ds(c % 8, 8, stride=8)
-        x_out[c // 8, to, :] = x[c] + alpha * (r[c] + beta * p[c])
-        r_out[c // 8, to, :] = r[c] - alpha * (w[c] + beta * s[c])
+    for c in range(16):
+        for k in range(4):
+            at, to = pl.ds(8 * k, 8), pl.ds(64 * k + c % 8, 8, stride=8)
+            x_out[c // 8, to, :] = x[c, at, :] + alpha * (r[c, at, :] + beta * p[c, at, :])
+            r_out[c // 8, to, :] = r[c, at, :] - alpha * (w[c, at, :] + beta * s[c, at, :])
 
 
 def finish(scale, *fields):
-    of = pl.BlockSpec((64, 8, 128), lambda k: (0, k, 0))
-    to = pl.BlockSpec((8, 64, 128), lambda k: (0, k, 0))
+    of = pl.BlockSpec((16, 32, 128), lambda k: (k, 0, 0))
+    to = pl.BlockSpec((2, 256, 128), lambda k: (k, 0, 0))
     x, r = pl.pallas_call(
         finish_kernel,
         grid=(4,),
@@ -719,7 +742,7 @@
         step_kernel,
         out_shape=[
             *[jax.ShapeDtypeStruct((64, 32, 128), F32)] * 5,
-            jax.ShapeDtypeStruct((8, 128), F32),
+            jax.ShapeDtypeStruct((1, 1), F32),
             jax.ShapeDtypeStruct((16, 128), F32),
         ],
         in_specs=[pl.BlockSpec(memory_space=pl.ANY)] * 9,
@@ -733,8 +756,8 @@
             vm(1024, 128, dtype=BF16), vm(32, 128, 256, dtype=BF16),
             slot(I32), slot(I32), slot(I32), slot(I32), vm(32, 128, dtype=I32), vm(32, 128, dtype=I32),
             slot(), slot(), vm(128, 128),
-            slot(), slot(), slot(), slot(), slot(), vm(4096, 64), vm(1024, 1024, dtype=BF16),
-            field(), field(), vm(128, 64), slot(), vm(MEMBERS, 64, 128, dtype=I32),
+            vm(32, 128), vm(32, 128), vm(32, 128), vm(32, 128), vm(32, 128), vm(4096, 64), vm(1024, 1024, dtype=BF16),
+            field(), field(), vm(128, 64), slot(), vm(32, 128, dtype=I32), vm(8, 128, dtype=I32), vm(8, 128, dtype=I32), vm(128, 128, dtype=BF16),
             vm(ROUNDS, 128, 128), vm(ROUNDS, 128, 128), vm(128, 8, 256), vm(128, 8, 256),
             pltpu.SemaphoreType.DMA((9,)),
             pltpu.SemaphoreType.DMA((ROUNDS,)),

time: 83 us -> 75.1 us (0.905)
  Pallas kernels: 80.2 us -> 73.5 us
  local copies, waits for them, and re-layouts: 1.21 us -> 0.01 us
    pallas_call x1, Pallas kernels: 75.7 us -> 69 us  [shards(): pl.pallas_call(step_kernel, out_shape=[*[jax.ShapeDtypeStruct((64, 32, 12...]
    slice x1 -> x0, local copies, waits for them, and re-layouts: 1.2 us -> none  [shards(): flag[0, 0] > 0.5]
where the time goes in v4:
time: 75.1 us; the launch traced here: 74.9 us
  Pallas kernels  73.5 us (98%)
  between operations  1.37 us (2%)
    pallas_call x1, Pallas kernels, shards(): pl.pallas_call(step_kernel, out_shape=[*[jax.ShapeDtypeStruct((64, 32, 12...  69 us
    pallas_call x1, Pallas kernels, finish(): pl.pallas_call(finish_kernel, grid=(4,), out_shape=[jax.ShapeDtypeStruct(...  4.48 us

profile of v4, /device:TPU:1, one launch (start us, length us, event | category | flops | bytes accessed | tf_op | source)
XLA Modules:
  0.0 74.9 jit_solution(11610095642073827736)
XLA Ops:
  0.6 0.0 copy-start.34
  0.6 0.0 copy-start.24
  0.7 0.0 copy-start.38
  0.7 69.0 %shard_map.108 = (f32[64,32,128]{2,1,0:T(8,128)}, f32[64,32,128]{2,1,0:T(8,128)}, f32[64,32,128]{2,1,0:T(8,128)}, f32[64,32,128]{2,1,0:T(8,128)}, f32[64,32,128]...) custom-call(f32[2048,128]{1,0:T(8,128)} %bitcast.124, f32[2048,128]{1,0:T(8,128)} %bitcast.131, ...), custom_call_target="tpu_custom_call" | custom-call | tf_op jit(solution)/shard_map/pallas_call | solution.py:741
  70.4 0.0 copy-done.34
  70.4 0.0 copy-done.24
  70.4 0.0 copy-done.38
  70.4 4.5 %conditional.1 = (f32[64,4096]{1,0:T(8,128)}, f32[64,4096]{1,0:T(8,128)}) conditional(s32[]{:T(128)} %bitcast.55, (f32[16,128]{1,0:T(8,128)S(1)}, f32[64,32,128]{2,1,0:T(8,128)}, f32[64,32,128]{2,1,0:T(8,128)}, f32[64,32,128]{2,1,0:T(8,128)}, f32[64,32,128]{2,1,0:T(8,128)}, /*index=5*/f32[64,32,128]{2,1,0:T(8,128)}) %tuple.27, ...), branch_computations={%region_0.0_spmd, %region_1.22_spmd} | conditional | flops 3247519744 | bytes 288816960 | solution.py:776
  70.4 4.5 %branch_0_fun.1 = (f32[8,256,128]{2,1,0:T(8,128)}, f32[8,256,128]{2,1,0:T(8,128)}) custom-call(f32[16,128]{1,0:T(8,128)S(1)} %get-tuple-element.165.scale, f32[64,32,128]{2,1,0:T(8,128)} %get-tuple-element.166.x, f32[64,32,128]{2,1,0:T(8,128)} %get-tuple-element.167.r, f32[64,32,128]{2,1,0:T(8,128)} %get-tuple-element.168.p, ...), custom_call_target="tpu_custom_call" | custom-call | tf_op jit(solution)/shard_map/cond/branch_0_fun/pallas_call | solution.py:714
Async XLA Ops:
  0.6 69.7 %copy-start.34 = (s32[4096]{0:T(1024)S(1)}, s32[4096]{0:T(1024)}, u32[]{:S(2)}) copy-start(s32[4096]{0:T(1024)} %param.16) | copy-start | bytes 49156
  0.6 69.7 %copy-start.24 = (f32[1,256,256]{2,1,0:T(8,128)S(1)}, f32[1,256,256]{2,1,0:T(8,128)}, u32[]{:S(2)}) copy-start(f32[1,256,256]{2,1,0:T(8,128)} %param.19) | copy-start | bytes 786436
  0.7 69.7 %copy-start.38 = (s32[1,256,1]{1,2,0:T(1,128)S(1)}, s32[1,256,1]{1,2,0:T(1,128)}, u32[]{:S(2)}) copy-start(s32[1,256,1]{1,2,0:T(1,128)} %param.20) | copy-start | bytes 3076

commit v5 on v4

--- a/solution.py
+++ b/solution.py
@@ -398,7 +398,7 @@
             nat[pl.ds(64 * b, 64), :] = (o[0:64] + o[64:128]) + o[128:192]
             return c
 
-        lax.fori_loop(0, 32, one, 0, unroll=16)
+        lax.fori_loop(0, 32, one, 0, unroll=32)
 
     def stencil(k, load, emit, mass):
         at = pl.ds(8 * k, 8)

time: 75.1 us -> 74.4 us (level)
  no operation moved by 1% of the time
where the time goes in v5:
time: 74.4 us; the launch traced here: 74.2 us
  Pallas kernels  72.8 us (98%)
  between operations  1.37 us (2%)
    pallas_call x1, Pallas kernels, shards(): pl.pallas_call(step_kernel, out_shape=[*[jax.ShapeDtypeStruct((64, 32, 12...  68.3 us
    pallas_call x1, Pallas kernels, finish(): pl.pallas_call(finish_kernel, grid=(4,), out_shape=[jax.ShapeDtypeStruct(...  4.48 us

profile of v5, /device:TPU:1, one launch (start us, length us, event | category | flops | bytes accessed | tf_op | source)
XLA Modules:
  0.0 74.2 jit_solution(2539659528843856741)
XLA Ops:
  0.6 0.0 copy-start.34
  0.6 0.0 copy-start.24
  0.7 0.0 copy-start.38
  0.7 68.3 %shard_map.108 = (f32[64,32,128]{2,1,0:T(8,128)}, f32[64,32,128]{2,1,0:T(8,128)}, f32[64,32,128]{2,1,0:T(8,128)}, f32[64,32,128]{2,1,0:T(8,128)}, f32[64,32,128]...) custom-call(f32[2048,128]{1,0:T(8,128)} %bitcast.124, f32[2048,128]{1,0:T(8,128)} %bitcast.131, ...), custom_call_target="tpu_custom_call" | custom-call | tf_op jit(solution)/shard_map/pallas_call | solution.py:741
  69.7 0.0 copy-done.34
  69.7 0.0 copy-done.24
  69.7 0.0 copy-done.38
  69.7 4.5 %conditional.1 = (f32[64,4096]{1,0:T(8,128)}, f32[64,4096]{1,0:T(8,128)}) conditional(s32[]{:T(128)} %bitcast.55, (f32[16,128]{1,0:T(8,128)S(1)}, f32[64,32,128]{2,1,0:T(8,128)}, f32[64,32,128]{2,1,0:T(8,128)}, f32[64,32,128]{2,1,0:T(8,128)}, f32[64,32,128]{2,1,0:T(8,128)}, /*index=5*/f32[64,32,128]{2,1,0:T(8,128)}) %tuple.27, ...), branch_computations={%region_0.0_spmd, %region_1.22_spmd} | conditional | flops 3247519744 | bytes 288816960 | solution.py:776
  69.7 4.5 %branch_0_fun.1 = (f32[8,256,128]{2,1,0:T(8,128)}, f32[8,256,128]{2,1,0:T(8,128)}) custom-call(f32[16,128]{1,0:T(8,128)S(1)} %get-tuple-element.165.scale, f32[64,32,128]{2,1,0:T(8,128)} %get-tuple-element.166.x, f32[64,32,128]{2,1,0:T(8,128)} %get-tuple-element.167.r, f32[64,32,128]{2,1,0:T(8,128)} %get-tuple-element.168.p, ...), custom_call_target="tpu_custom_call" | custom-call | tf_op jit(solution)/shard_map/cond/branch_0_fun/pallas_call | solution.py:714
Async XLA Ops:
  0.6 69.0 %copy-start.34 = (s32[4096]{0:T(1024)S(1)}, s32[4096]{0:T(1024)}, u32[]{:S(2)}) copy-start(s32[4096]{0:T(1024)} %param.16) | copy-start | bytes 49156
  0.6 69.0 %copy-start.24 = (f32[1,256,256]{2,1,0:T(8,128)S(1)}, f32[1,256,256]{2,1,0:T(8,128)}, u32[]{:S(2)}) copy-start(f32[1,256,256]{2,1,0:T(8,128)} %param.19) | copy-start | bytes 786436
  0.7 69.0 %copy-start.38 = (s32[1,256,1]{1,2,0:T(1,128)S(1)}, s32[1,256,1]{1,2,0:T(1,128)}, u32[]{:S(2)}) copy-start(s32[1,256,1]{1,2,0:T(1,128)} %param.20) | copy-start | bytes 3076
